TPU v7x, 128 devices: a whole 4x4x4 slice. The times are simulated.
128 devices in a mesh: band: 16 (over y, x), ga: 8 (over z, core).
Axes of the slice: x: 4, y: 4, z: 4, core: 2. Of those that a mesh axis runs over, the one named last changes fastest.
Arguments:
- waves: bfloat16 [2, 128, 4, 147456], P(None, 'band', None, 'ga'), as said below
- ionic_field: float32 [384, 1536], P('ga'), may hold values from -1 to 3
- point_charge: float32 [32768], P(('band', 'ga')), may hold values from -6 to 6
- charge_place: float32 [3, 32768], P(None, ('band', 'ga')), may hold values from 0 to 1
- charge_slab: int32 [32768, 1], P(('band', 'ga')), may hold values from 0 to 7; in each aligned block of 256 rows (0 to 255, 256 to 511, ...) at most 128 rows name the same one
Outputs:
- applied_waves: bfloat16 [2, 128, 4, 147456], P(None, 'band', None, 'ga')
- subspace: float32 [2, 128, 128], P(None, 'band', 'ga')
Inputs may be any that keep to these rules, and one draw needn't show every extreme that they name: `waves`: entries are of order one. `charge_slab`: among the 256 rows of one device at most 128 name the same slab, and in every draw some device has exactly 128 rows naming one slab.
All inputs are finite; a program needn't handle non-finite values.
Results may differ from a plain program's by a relative error of at most 0.0073.
Values may be sent and summed in bfloat16 or wider, within the bound.
A program may use at most 128 MiB of HBM per device.

v0:
```python
import jax
import jax.numpy as jnp
from jax import lax
from jax.sharding import PartitionSpec as P

NX = 384
NY = 384


width_cells = 1.5


def tables(length):
    indices = jnp.arange(length, dtype=jnp.int32)
    phases = indices[:, None] * indices[None, :] % length
    angles = phases.astype(jnp.float32) * (2.0 * jnp.pi / length)
    factor = 1.0 / jnp.sqrt(jnp.float32(length))
    return jnp.stack([jnp.cos(angles) * factor, jnp.sin(angles) * factor]).astype(jnp.bfloat16)


def combine(products, sign_flip):
    return jnp.stack(
        [products[0, 0] - sign_flip * products[1, 1], sign_flip * products[0, 1] + products[1, 0]]
    )


def gaussian(distance):
    return jnp.exp(-distance * distance / (2.0 * width_cells * width_cells))


def frequency(indices, length):
    return jnp.where(indices < length // 2, indices, indices - length).astype(jnp.float32)


def atom_terms(charges, place_x, place_z, planes):
    cells_x = jnp.arange(NX, dtype=jnp.float32)
    plane_cells = jnp.arange(planes, dtype=jnp.float32)
    kernel_x = gaussian(cells_x[None, :] - NX * place_x[:, None])
    kernel_z = gaussian(plane_cells[None, :] - planes * place_z[:, None])
    return ((charges[:, None] * kernel_z)[:, :, None] * kernel_x[:, None, :]).reshape(
        charges.shape[0], planes * NX
    )


def shards(waves, ionic_field, point_charge, charge_place, charge_slab):
    ga_count = lax.axis_size("ga")
    band_groups = lax.axis_size("band")
    band_count = waves.shape[1]
    planes = waves.shape[2]
    rows_x = NX // ga_count
    slab_rows = NY // ga_count
    slab_index = lax.axis_index("ga")
    table_rows = tables(NX)
    table_cols = tables(NY)
    target = charge_slab[:, 0]
    cells_y = jnp.arange(NY, dtype=jnp.float32)
    along_y = target.astype(jnp.float32) * slab_rows + slab_rows * charge_place[1]
    inside = jnp.arange(NY, dtype=jnp.int32)[None, :] // slab_rows == target[:, None]
    kernel_y = gaussian(cells_y[None, :] - along_y[:, None]) * inside.astype(jnp.float32)
    right_side = atom_terms(point_charge, charge_place[0], charge_place[2], planes)
    term_grid = jnp.dot(
        kernel_y.T, right_side, precision=lax.Precision.HIGHEST, preferred_element_type=jnp.float32
    )
    whole_grid = lax.psum(term_grid, ("band", "ga"))
    charge_pot = lax.dynamic_slice_in_dim(whole_grid, slab_index * slab_rows, slab_rows, 0)
    potential = (ionic_field + charge_pot).reshape(slab_rows, planes, NX)
    row_global = slab_index * rows_x + jnp.arange(rows_x, dtype=jnp.int32)
    freq_x = frequency(row_global, NX)
    freq_y = frequency(jnp.arange(NY, dtype=jnp.int32), NY)
    kinetic = 2.0 * (
        freq_x[:, None] * freq_x[:, None] / (NX * NX)
        + freq_y[None, :] * freq_y[None, :] / (NY * NY)
    )
    waves_grid = waves.reshape(2, band_count, planes, rows_x, NY)
    half_done = combine(
        jnp.einsum(
            "cnpxy,tysk->ctnpsxk",
            waves_grid,
            table_cols.reshape(2, NY, ga_count, slab_rows),
            preferred_element_type=jnp.float32,
        ),
        1.0,
    ).astype(jnp.bfloat16)
    outgoing = half_done.reshape(2, band_count, planes, ga_count, rows_x * slab_rows)
    columns_in = lax.all_to_all(outgoing, "ga", split_axis=3, concat_axis=3, tiled=True).reshape(
        2, band_count, planes, NX, slab_rows
    )
    in_space = combine(
        jnp.einsum("cnpxy,txk->ctnypk", columns_in, table_rows, preferred_element_type=jnp.float32),
        1.0,
    )
    weighted = (potential * in_space).astype(jnp.bfloat16)
    return_half = combine(
        jnp.einsum(
            "cnypx,txsk->ctnpsyk",
            weighted,
            table_rows.reshape(2, NX, ga_count, rows_x),
            preferred_element_type=jnp.float32,
        ),
        -1.0,
    ).astype(jnp.bfloat16)
    rows_recv = lax.all_to_all(
        return_half.reshape(2, band_count, planes, ga_count, slab_rows * rows_x),
        "ga",
        split_axis=3,
        concat_axis=3,
        tiled=True,
    ).reshape(2, band_count, planes, NY, rows_x)
    recip_part = combine(
        jnp.einsum("cnpyx,tyk->ctnpxk", rows_recv, table_cols, preferred_element_type=jnp.float32),
        -1.0,
    )
    applied_waves = (
        (kinetic * waves_grid.astype(jnp.float32) + recip_part)
        .astype(jnp.bfloat16)
        .reshape(2, band_count, planes, rows_x * NY)
    )
    inverse_cells = 1.0 / (planes * NX * NY)
    waves_band, applied_band = (
        lax.all_to_all(waves, "band", split_axis=3, concat_axis=1, tiled=True),
        lax.all_to_all(applied_waves, "band", split_axis=3, concat_axis=1, tiled=True),
    )
    products = jnp.einsum(
        "cnpg,dmpg->cdnm", waves_band, applied_band, preferred_element_type=jnp.float32
    )
    full_matrix = (
        jnp.stack([products[0, 0] + products[1, 1], products[0, 1] - products[1, 0]])
        * inverse_cells
    )
    all_bands = band_count * band_groups
    col_width = all_bands // ga_count
    blocks = full_matrix.reshape(2, band_groups, band_count, ga_count, col_width)
    blocks = blocks.transpose(1, 3, 0, 2, 4).reshape(
        band_groups * ga_count, 2, band_count, col_width
    )
    subspace = lax.psum_scatter(blocks, ("band", "ga"), scatter_dimension=0, tiled=True)[0]
    return (applied_waves, subspace)


def solution(mesh):
    placed = (
        P(None, "band", None, "ga"),
        P("ga", None),
        P(("band", "ga")),
        P(None, ("band", "ga")),
        P(("band", "ga"), None),
    )
    return jax.shard_map(
        shards,
        mesh=mesh,
        in_specs=placed,
        out_specs=(P(None, "band", None, "ga"), P(None, "band", "ga")),
        check_vma=False,
    )
```

profile of v0, /device:TPU:1, one launch (start us, length us, event | category | flops | bytes accessed | tf_op | source)
XLA Modules:
  0.0 1340.4 jit_solution(9864846055614011837)
XLA Ops:
  10.1 3.4 reshape.518
  13.5 10.9 convolution_bitcast_fusion.1
  24.4 12.4 fusion.4
  36.7 3.4 copy.92
  40.2 3.8 sub.146
  47.4 3.8 add.182
  55.6 7.0 all-to-all-start
  63.4 3.7 fusion.47
  67.1 3.7 multiply_convert_fusion.2
  70.9 153.7 %all-reduce.2.cloned.1.call-done = f32[384,1536]{1,0:T(8,128)} async-done(((f32[384,1536]{1,0:T(8,128)}), f32[384,1536]{1,0:T(8,128)}) %all-reduce.2.cloned.1.call-update) | async-done | bytes 2359312 | tf_op jit(solution)/shard_map/psum | solution.py:64
  228.3 10.9 reshape.514
  239.2 5.1 fusion.11
  245.6 10.9 convolution_bitcast_fusion
  256.5 12.4 fusion.2
  272.3 3.8 sub.150
  279.6 3.8 add.186
  287.7 5.5 all-to-all-start.1
  293.3 35.9 %copy.108 = bf16[2,8,4,18432]{1,2,0,3:T(4,128)(2,1)} copy(bf16[2,8,4,18432]{3,2,1,0:T(4,128)(2,1)S(1)} %copy-done) | data formatting | bytes 4718592 | tf_op args[0]
  329.2 43.4 %reshape.527 = bf16[16,2,36864]{2,1,0:T(2,128)(2,1)} reshape(bf16[18432,2,4,8]{3,2,1,0:T(4,128)(2,1)} %bitcast.125) | data formatting | bytes 4718592
  372.8 5.1 all-to-all-start.3
  377.9 4.4 copy.102
  382.3 10.9 reshape.515
  393.2 5.1 fusion.14
  404.5 4.5 copy.104
  418.6 39.6 %copy.106 = bf16[2,8,4,18432]{1,2,0,3:T(4,128)(2,1)} copy(bf16[2,8,4,18432]{3,1,2,0:T(8,128)(2,1)} %fusion.10) | data formatting | bytes 4718592 | tf_op jit(solution)/shard_map/convert_element_type | solution.py:115
  458.1 43.6 %reshape.529 = bf16[16,2,36864]{2,1,0:T(2,128)(2,1)} reshape(bf16[18432,2,4,8]{3,2,1,0:T(4,128)(2,1)} %bitcast.128) | data formatting | bytes 4718592
  501.7 6.6 all-to-all-start.2
  508.4 45.9 %reshape.528 = bf16[18432,2,4,8]{3,2,1,0:T(4,128)(2,1)} reshape(bf16[16,2,36864]{2,1,0:T(2,128)(2,1)} %all-to-all-done.3) | data formatting | bytes 4718592
  554.3 46.7 %copy.109 = bf16[2,8,4,16,1152]{4,1,3,2,0:T(8,128)(2,1)} copy(bf16[2,8,4,16,1152]{1,2,0,4,3:T(4,128)(2,1)} %bitcast.126) | data formatting | bytes 4718592 | tf_op jit(solution)/shard_map/all_to_all | solution.py:120
  601.0 46.5 %reshape.530 = bf16[18432,2,4,8]{3,2,1,0:T(4,128)(2,1)} reshape(bf16[16,2,36864]{2,1,0:T(2,128)(2,1)S(1)} %all-to-all-done.2) | data formatting | bytes 4718592
  647.5 46.8 %copy.107 = bf16[2,8,4,16,1152]{4,1,3,2,0:T(8,128)(2,1)} copy(bf16[2,8,4,16,1152]{1,2,0,4,3:T(4,128)(2,1)} %bitcast.127) | data formatting | bytes 4718592 | tf_op jit(solution)/shard_map/all_to_all | solution.py:121
  702.7 630.6 %reduce-scatter.2.cloned.1.call-done = f32[1,2,8,16]{3,2,1,0:T(8,128)} async-done(((f32[128,2,8,16]{3,2,1,0:T(8,128)}), f32[1,2,8,16]{3,2,1,0:T(8,128)}) %reduce-scatter.2.cloned.1.call-update) | async-done | bytes 1040 | tf_op jit(solution)/shard_map/reduce_scatter | solution.py:136
  (78 shorter events, 51.9 us)
Async XLA Ops:
  10.0 3.5 copy-start.3
  55.6 7.0 copy-start.12
  55.6 7.0 copy-start.11
  55.6 7.0 copy-start.13
  55.6 170.0 %all-to-all-start = ((bf16[2,8,4,8,2304]{4,2,1,0,3:T(4,128)(2,1)}), bf16[2,8,4,8,2304]{4,2,1,0,3:T(4,128)(2,1)S(1)}, u32[]{:S(2)}, u32[]{:S(2)}) async-start(bf16[2,8,4,8,2304]{4,2,1,0,3:T(4,128)(2,1)} %copy.94), calls=%async_computation | async-start | bytes 4718592 | tf_op jit(solution)/shard_map/all_to_all | solution.py:85
  62.5 162.0 %all-reduce.2.cloned.1.call-start = ((), (), s32[]{:S(2)}) async-start(), calls=%async_computation.5 | async-start | bytes 4718592 | tf_op jit(solution)/shard_map/psum | solution.py:64
  67.1 157.5 %copy-start.6 = (f32[48,1536]{1,0:T(8,128)S(1)}, f32[48,1536]{1,0:T(8,128)}, u32[]{:S(2)}) copy-start(f32[48,1536]{1,0:T(8,128)} %param.6) | copy-start | bytes 884740
  228.3 10.9 copy-start.7
  228.3 10.9 copy-start.9
  244.6 1.0 copy-start.4
  287.7 5.6 copy-start
  287.7 85.1 %all-to-all-start.1 = ((bf16[2,8,4,8,2304]{4,2,1,0,3:T(4,128)(2,1)}), bf16[2,8,4,8,2304]{4,2,1,0,3:T(4,128)(2,1)}, u32[]{:S(2)}, u32[]{:S(2)}) async-start(bf16[2,8,4,8,2304]{4,2,1,0,3:T(4,128)(2,1)} %copy.101), calls=%async_computation.1 | async-start | bytes 4718592 | tf_op jit(solution)/shard_map/all_to_all | solution.py:102
  372.8 128.9 %all-to-all-start.3 = ((bf16[16,2,36864]{2,1,0:T(2,128)(2,1)}), bf16[16,2,36864]{2,1,0:T(2,128)(2,1)}, u32[]{:S(2)}, u32[]{:S(2)}) async-start(bf16[16,2,36864]{2,1,0:T(2,128)(2,1)} %reshape.527), calls=%async_computation.3 | async-start | bytes 4718592 | tf_op jit(solution)/shard_map/all_to_all | solution.py:120
  382.3 10.9 copy-start.8
  382.3 10.9 copy-start.10
  412.3 3.2 copy-start.2
  501.7 99.2 %all-to-all-start.2 = ((bf16[16,2,36864]{2,1,0:T(2,128)(2,1)}), bf16[16,2,36864]{2,1,0:T(2,128)(2,1)S(1)}, u32[]{:S(2)}, u32[]{:S(2)}) async-start(bf16[16,2,36864]{2,1,0:T(2,128)(2,1)} %reshape.529), calls=%async_computation.2 | async-start | bytes 4718592 | tf_op jit(solution)/shard_map/all_to_all | solution.py:121
  508.3 825.0 %reduce-scatter.2.cloned.1.call-start = ((), (), s32[]{:S(2)}) async-start(), calls=%async_computation.6 | async-start | bytes 1056768 | tf_op jit(solution)/shard_map/reduce_scatter | solution.py:136
  647.5 46.8 %copy-start.5 = (bf16[2,8,4,16,1152]{4,1,3,2,0:T(8,128)(2,1)S(1)}, bf16[2,8,4,16,1152]{4,1,3,2,0:T(8,128)(2,1)}, u32[]{:S(2)}) copy-start(bf16[2,8,4,16,1152]{4,1,3,2,0:T(8,128)(2,1)} %copy.109) | copy-start | bytes 7077892
  697.4 2.0 copy-start.1
Sparse Core Ops, SparseCore 0:
  68.1 156.4 all-reduce.1
  698.9 634.3 reduce-scatter.1
where the time goes:
time: 1360 us; the launch traced here: 1340 us
  waiting for transfers between devices  784 us (58%)
  local copies, waits for them, and re-layouts  436 us (32%)
  other arithmetic  43.3 us (3%)
  matrix products  38.1 us (3%)
  starting transfers between devices  24.3 us (2%)
  between operations  14.6 us (1%)
    reduce_scatter x1, waiting for transfers between devices, shards(): lax.psum_scatter(blocks, ('band', 'ga'), scatter_dimension=0, tiled=True)[0]  631 us
    unnamed x35, local copies, waits for them, and re-layouts  220 us
    psum x1, waiting for transfers between devices, shards(): whole_grid = lax.psum(term_grid, ('band', 'ga'))  154 us
    all_to_all x1, local copies, waits for them, and re-layouts, shards(): lax.all_to_all(applied_waves, 'band', split_axis=3, concat_axis=1, tiled=...  46.8 us
    all_to_all x1, local copies, waits for them, and re-layouts, shards(): lax.all_to_all(waves, 'band', split_axis=3, concat_axis=1, tiled=True)  46.7 us
    convert_element_type x1, local copies, waits for them, and re-layouts, shards(): applied_waves = (kinetic * waves_grid.astype(jnp.float32) + recip_part).a...  39.6 us
    another operation x4, other arithmetic  31.4 us
  transfers between devices with their start and end apart: 6, of which 2 were waited for; matrix products, arithmetic and copies ran while one was open for 23% of the time, Pallas kernels for 0%

commit v1 on v0

v1 whole, which is shorter than its diff:
```python
import functools

import jax
import jax.numpy as jnp
import ml_dtypes
import numpy as np
from jax import lax
from jax.experimental import pallas as pl
from jax.experimental.pallas import tpu as pltpu
from jax.sharding import PartitionSpec as P

N = 384
ROWS = 48
BF = jnp.bfloat16
F32 = jnp.float32
MESH = pl.DeviceIdType.MESH


def tables():
    indices = np.arange(N, dtype=np.int32)
    phases = indices[:, None] * indices[None, :] % N
    angles = phases.astype(np.float32) * np.float32(2.0 * np.pi / N)
    factor = np.float32(1.0) / np.sqrt(np.float32(N))
    return np.stack([np.cos(angles) * factor, np.sin(angles) * factor]).astype(ml_dtypes.bfloat16)


def dot(a, b):
    return jnp.dot(a, b, preferred_element_type=F32)


def dot_nt(a, b):
    return lax.dot_general(a, b, (((1,), (1,)), ((), ())), preferred_element_type=F32)


def split(value):
    high = value.astype(BF)
    return high, (value - high.astype(F32)).astype(BF)


def gaussian(distance):
    return jnp.exp(-distance * distance / 4.5)


def kernel(
    w1, charges, ionic, tab, out, sub,
    m1, m2, perm, kin, zb, w2, xw, phi, ph, p2, xp, ab, fs, ts, bs,
    ch, io, pot, rsb, pf, vyx, vxy, gt, sa, st, sb,
    zi_s, zi_r, zo_s, zo_r, ch_s, ch_r, io_s, io_r, rs_s, rs_r, ag_s, ag_r,
    sp_s, sp_r, sf_s, sf_r, xw_s, xw_r, xp_s, xp_r, sa_s, sa_r, sb_s, sb_r, loc,
):
    b = lax.axis_index("band")
    g = lax.axis_index("ga")
    z = g // 2
    h = lax.rem(g, 2)
    sibling = g + 1 - 2 * h

    def ga_peer(k):
        return lax.rem(g + k, 8)

    def band_peer(k):
        return lax.rem(b + k, 16)

    def remote(src, dst, send, recv, band, ga):
        return pltpu.make_async_remote_copy(
            src_ref=src, dst_ref=dst, send_sem=send, recv_sem=recv,
            device_id=(band, ga), device_id_type=MESH,
        )

    def at(start, size, step):
        return pl.ds(pl.multiple_of(start * size, step), size)

    barrier = pltpu.get_barrier_semaphore()

    def greet_ga(k, c):
        pl.semaphore_signal(barrier, inc=1, device_id=(b, ga_peer(k)), device_id_type=MESH)
        return c

    def greet_band(k, c):
        pl.semaphore_signal(barrier, inc=1, device_id=(band_peer(k), g), device_id_type=MESH)
        return c

    lax.fori_loop(1, 8, greet_ga, 0)
    lax.fori_loop(1, 16, greet_band, 0)
    pl.semaphore_wait(barrier, 22)

    def ch_copy(source, target):
        return remote(charges, ch.at[source], ch_s.at[target], ch_r.at[source], b, target)

    def io_copy(source, target):
        return remote(
            ionic.at[:, at(target // 2, N, 128)], io.at[at(source, ROWS, 8), :],
            io_s.at[target], io_r.at[source], b, target,
        )

    def zi_copy(n, source, target):
        return remote(
            w1.at[:, 4 * lax.rem(target, 2) + n, target // 2],
            zb.at[:, n, at(source, ROWS, 16), :],
            zi_s.at[n, target], zi_r.at[n, source], b, target,
        )

    def zo_copy(n, source, target):
        return remote(
            ab.at[:, n, at(target, ROWS, 16), :],
            out.at[:, 4 * lax.rem(source, 2) + n, source // 2],
            zo_s.at[n, target], zo_r.at[n, source], b, target,
        )

    def xw_copy(source, target):
        return remote(
            w2.at[at(target, 12, 1)], xw.at[:, at(source, 16, 16), :],
            xw_s.at[target], xw_r.at[source], target, g,
        )

    def xp_copy(source, target):
        return remote(
            p2.at[at(target, 12, 1)], xp.at[:, at(source, 16, 16), :],
            xp_s.at[target], xp_r.at[source], target, g,
        )

    def rs_copy(source, target):
        return remote(
            pot.at[at(target, 16, 8), :], rsb.at[source],
            rs_s.at[target], rs_r.at[source], target, g,
        )

    def ag_copy(source, target):
        piece = at(source, 16, 8)
        return remote(
            pf.at[h, piece, :], pf.at[h, piece, :],
            ag_s.at[target], ag_r.at[source], target, g,
        )

    def sp_copy(half):
        return remote(pf.at[half], pf.at[half], sp_s.at[0], sp_r.at[0], b, sibling)

    def sf_copy(n, core):
        return remote(
            phi.at[n, :, at(1 - core, 192, 16), :], ph.at[:, 4 * core + n],
            sf_s.at[n], sf_r.at[n], b, sibling,
        )

    def sa_copy(source, target):
        return remote(
            gt.at[at(target, 32, 8), :], sa.at[source],
            sa_s.at[target], sa_r.at[source], b, target,
        )

    def sb_copy(source, target):
        return remote(
            st.at[at(target, 16, 8), :], sb.at[source],
            sb_s.at[target], sb_r.at[source], target, g,
        )

    def each(low, high, body):
        def step(k, c):
            body(k)
            return c

        lax.fori_loop(low, high, step, 0)

    each(1, 8, lambda k: ch_copy(g, ga_peer(k)).start())
    each(1, 8, lambda k: zi_copy(0, g, ga_peer(k)).start())
    each(1, 8, lambda k: io_copy(g, ga_peer(k)).start())
    for n in range(1, 4):
        each(1, 8, lambda k, n=n: zi_copy(n, g, ga_peer(k)).start())

    def zi_own(n):
        return pltpu.make_async_copy(
            w1.at[:, 4 * h + n, z], zb.at[:, n, at(g, ROWS, 16), :], loc.at[n]
        )

    for n in range(4):
        zi_own(n).start()

    c = tab[0]
    s = tab[1]
    m1[0:N, 0:N] = c
    m1[0:N, N : 2 * N] = s
    m1[N : 2 * N, 0:N] = -s
    m1[N : 2 * N, N : 2 * N] = c
    m2[0:N, 0:N] = c
    m2[0:N, N : 2 * N] = -s
    m2[N : 2 * N, 0:N] = s
    m2[N : 2 * N, N : 2 * N] = c
    to = lax.broadcasted_iota(jnp.int32, (256, 256), 0)
    of = lax.broadcasted_iota(jnp.int32, (256, 256), 1)
    perm[...] = jnp.where(
        ((to >> 4) == (of & 15)) & ((to & 15) == (of >> 4)), 1.0, 0.0
    ).astype(BF)

    def frequency(indices):
        return jnp.where(indices < N // 2, indices, indices - N).astype(F32)

    fx = frequency(lax.broadcasted_iota(jnp.int32, (N, N), 0))
    fy = frequency(lax.broadcasted_iota(jnp.int32, (N, N), 1))
    kin[...] = 2.0 * (fx * fx / (N * N) + fy * fy / (N * N))

    for p in range(4):
        def turn(x, p=p):
            block = w1[:, :, p, at(x, 16, 16), :].reshape(256, N)
            turned = dot(perm[...], block).astype(BF).reshape(16, 16, N)
            w2[pl.ds(ROWS * p + 16 * x, 16)] = turned

        each(0, 3, turn)

    each(1, 8, lambda k: ch_copy(ga_peer(k), g).wait_recv())
    ch[g] = charges[...]
    pot[...] = jnp.zeros((256, N), F32)

    def add_charges(source):
        rows = ch[source]
        q, u, v, w, slab = (rows[i : i + 1] for i in range(5))
        r = lax.broadcasted_iota(jnp.int32, (256, 256), 0)
        y = 192 * h + 12 * (r >> 4) + (r & 15)
        weight = q * gaussian(z.astype(F32) - 4.0 * w)
        inside = ((y * 1366) >> 16).astype(F32) == slab
        gy = gaussian(y.astype(F32) - (slab * 48.0 + 48.0 * v)) * weight
        gy = jnp.where(inside, gy, 0.0)
        x = lax.broadcasted_iota(jnp.int32, (N, 256), 0).astype(F32)
        gx = gaussian(x - 384.0 * u)
        yh, yl = split(gy)
        xh, xl = split(gx)
        pot[...] += dot_nt(yh, xh) + (dot_nt(yh, xl) + dot_nt(yl, xh))

    each(0, 8, add_charges)
    each(1, 16, lambda k: rs_copy(b, band_peer(k)).start())

    def xw_own():
        return pltpu.make_async_copy(
            w2.at[at(b, 12, 1)], xw.at[:, at(b, 16, 16), :], loc.at[4]
        )

    xw_own().start()
    each(1, 4, lambda k: xw_copy(b, band_peer(k)).start())

    each(1, 16, lambda k: rs_copy(band_peer(k), b).wait_recv())
    piece = pot[at(b, 16, 8), :]
    for k in range(1, 16):
        piece = piece + rsb[band_peer(k)]
    pf[h, at(b, 16, 8), :] = piece
    each(1, 16, lambda k: ag_copy(b, band_peer(k)).start())
    each(4, 16, lambda k: xw_copy(b, band_peer(k)).start())
    each(1, 16, lambda k: ag_copy(band_peer(k), b).wait_recv())
    sp_copy(h).start()
    each(1, 8, lambda k: io_copy(ga_peer(k), g).wait_recv())
    io[at(g, ROWS, 8), :] = ionic[:, at(z, N, 128)]
    sp_copy(1 - h).wait_recv()
    for half in range(2):
        def place(q, half=half):
            two = pf[half, at(q, 32, 8), :]
            dst = pl.ds(pl.multiple_of(192 * half + 24 * q, 8), 24)
            vyx[dst, :] = io[dst, :] + jnp.concatenate([two[0:12], two[16:28]], axis=0)

        each(0, 8, place)
    vxy[...] = vyx[...].T

    def plane(n):
        each(1, 8, lambda k: zi_copy(n, ga_peer(k), g).wait_recv())
        zi_own(n).wait()
        both = jnp.concatenate([zb[0, n], zb[1, n]], axis=1)
        fs[0:N] = dot(both, m1[:, 0:N]).astype(BF)
        fs[N : 2 * N] = dot(both, m1[:, N : 2 * N]).astype(BF)
        for part in range(2):
            space = dot(m2[part * N : (part + 1) * N], fs[...])
            phi[n, part] = space.astype(BF)
            ts[part * N : (part + 1) * N] = (space * vxy[...]).astype(BF)
        sf_copy(n, h).start()
        for part in range(2):
            ph[part, 4 * h + n] = phi[n, part, at(h, 192, 16), :]
        for part in range(2):
            bs[:, part * N : (part + 1) * N] = dot(
                m1[part * N : (part + 1) * N], ts[...]
            ).astype(BF)
        for part in range(2):
            recip = dot(bs[...], m2[:, part * N : (part + 1) * N])
            ab[part, n] = (kin[...] * zb[part, n].astype(F32) + recip).astype(BF)
        each(1, 8, lambda k: zo_copy(n, g, ga_peer(k)).start())
        zo_own(n).start()

    def zo_own(n):
        return pltpu.make_async_copy(
            ab.at[:, n, at(g, ROWS, 16), :], out.at[:, 4 * h + n, z], loc.at[5 + n]
        )

    each(0, 4, plane)

    each(0, 4, lambda n: sf_copy(n, 1 - h).wait_recv())

    def turn_field(x):
        block = ph[:, :, at(x, 16, 16), :].reshape(256, N)
        p2[at(x, 16, 16)] = dot(perm[...], block).astype(BF).reshape(16, 16, N)

    each(0, 12, turn_field)

    def xp_own():
        return pltpu.make_async_copy(
            p2.at[at(b, 12, 1)], xp.at[:, at(b, 16, 16), :], loc.at[9]
        )

    each(1, 16, lambda k: xp_copy(b, band_peer(k)).start())
    xp_own().start()

    gt[...] = jnp.zeros((256, 256), F32)
    each(1, 16, lambda k: xw_copy(band_peer(k), b).wait_recv())
    xw_own().wait()

    def gram(rows, weight):
        gt[...] += dot_nt((rows.astype(F32) * weight).astype(BF), rows)

    def gram_waves(i):
        x = ROWS * g + lax.rem(12 * b + i, ROWS)
        gram(xw[i], kin[pl.ds(x, 1), :])

    each(0, 12, gram_waves)
    each(1, 16, lambda k: xp_copy(band_peer(k), b).wait_recv())
    xp_own().wait()
    each(0, 12, lambda i: gram(xp[i], vxy[pl.ds(192 * h + 12 * b + i, 1), :]))

    each(1, 8, lambda k: sa_copy(g, ga_peer(k)).start())
    total = gt[at(g, 32, 8), :]
    each(1, 8, lambda k: sa_copy(ga_peer(k), g).wait_recv())
    for k in range(1, 8):
        total = total + sa[ga_peer(k)]
    st[...] = jnp.concatenate([total, jnp.zeros((96, 256), F32)], axis=0).T
    each(1, 16, lambda k: sb_copy(b, band_peer(k)).start())
    block = st[at(b, 16, 8), :]
    each(1, 16, lambda k: sb_copy(band_peer(k), b).wait_recv())
    for k in range(1, 16):
        block = block + sb[band_peer(k)]
    row = lax.broadcasted_iota(jnp.int32, (128, 128), 0)
    col = lax.broadcasted_iota(jnp.int32, (128, 128), 1)
    lane = ((col >> 3) << 4) + (col & 7)
    valid = col < 16
    pick_re = jnp.where(valid & (row == lane), 1.0, 0.0)
    pick_im = jnp.where(valid & (row == lane + 8), 1.0, 0.0)

    def pick(rows, which):
        return jnp.dot(rows, which, precision=lax.Precision.HIGHEST, preferred_element_type=F32)

    inverse_cells = 1.0 / (4 * N * N)
    rr, ri = pick(block, pick_re), pick(block, pick_im)
    sub[0] = (rr[0:8] + ri[8:16]) * inverse_cells
    sub[1] = (ri[0:8] - rr[8:16]) * inverse_cells

    for n in range(4):
        each(1, 8, lambda k, n=n: zo_copy(n, ga_peer(k), g).wait_recv())
        each(1, 8, lambda k, n=n: zi_copy(n, g, ga_peer(k)).wait_send())
        each(1, 8, lambda k, n=n: zo_copy(n, g, ga_peer(k)).wait_send())
        zo_own(n).wait()
        sf_copy(n, h).wait_send()

    def ga_sent(k):
        ch_copy(g, ga_peer(k)).wait_send()
        io_copy(g, ga_peer(k)).wait_send()
        sa_copy(g, ga_peer(k)).wait_send()

    def band_sent(k):
        rs_copy(b, band_peer(k)).wait_send()
        ag_copy(b, band_peer(k)).wait_send()
        xw_copy(b, band_peer(k)).wait_send()
        xp_copy(b, band_peer(k)).wait_send()
        sb_copy(b, band_peer(k)).wait_send()

    each(1, 8, ga_sent)
    each(1, 16, band_sent)
    sp_copy(h).wait_send()


def shards(table, waves, ionic_field, point_charge, charge_place, charge_slab):
    w1 = waves.reshape(2, 8, 4, ROWS, N)
    charges = jnp.concatenate(
        [
            point_charge[None, :],
            charge_place,
            charge_slab.reshape(1, 256).astype(F32),
            jnp.zeros((3, 256), F32),
        ],
        axis=0,
    )
    dma = pltpu.SemaphoreType.DMA
    vmem = pltpu.VMEM
    out, sub = pl.pallas_call(
        kernel,
        out_shape=(
            jax.ShapeDtypeStruct((2, 8, 4, ROWS, N), BF),
            jax.ShapeDtypeStruct((2, 8, 128), F32),
        ),
        in_specs=[pl.BlockSpec(memory_space=pltpu.VMEM)] * 4,
        out_specs=(
            pl.BlockSpec(memory_space=pl.ANY),
            pl.BlockSpec(memory_space=pltpu.VMEM),
        ),
        scratch_shapes=[
            vmem((2 * N, 2 * N), BF),
            vmem((2 * N, 2 * N), BF),
            vmem((256, 256), BF),
            vmem((N, N), F32),
            vmem((2, 4, N, N), BF),
            vmem((192, 16, N), BF),
            vmem((12, 256, N), BF),
            vmem((4, 2, N, N), BF),
            vmem((2, 8, 192, N), BF),
            vmem((192, 16, N), BF),
            vmem((12, 256, N), BF),
            vmem((2, 4, N, N), BF),
            vmem((2 * N, N), BF),
            vmem((2 * N, N), BF),
            vmem((N, 2 * N), BF),
            vmem((8, 8, 256), F32),
            vmem((N, N), F32),
            vmem((256, N), F32),
            vmem((16, 16, N), F32),
            vmem((2, 256, N), F32),
            vmem((N, N), F32),
            vmem((N, N), F32),
            vmem((256, 256), F32),
            vmem((8, 32, 256), F32),
            vmem((256, 128), F32),
            vmem((16, 16, 128), F32),
            dma((4, 8)), dma((4, 8)),
            dma((4, 8)), dma((4, 8)),
            dma((8,)), dma((8,)),
            dma((8,)), dma((8,)),
            dma((16,)), dma((16,)),
            dma((16,)), dma((16,)),
            dma((1,)), dma((1,)),
            dma((4,)), dma((4,)),
            dma((16,)), dma((16,)),
            dma((16,)), dma((16,)),
            dma((8,)), dma((8,)),
            dma((16,)), dma((16,)),
            dma((10,)),
        ],
        compiler_params=pltpu.CompilerParams(
            collective_id=0, has_side_effects=True, vmem_limit_bytes=56 * 1024 * 1024
        ),
    )(w1, charges, ionic_field, table)
    return out.reshape(2, 8, 4, ROWS * N), sub[:, :, :16]


def solution(mesh):
    placed = (
        P(None, "band", None, "ga"),
        P("ga", None),
        P(("band", "ga")),
        P(None, ("band", "ga")),
        P(("band", "ga"), None),
    )
    mapped = jax.shard_map(
        shards,
        mesh=mesh,
        in_specs=(P(None, None, None),) + placed,
        out_specs=(P(None, "band", None, "ga"), P(None, "band", "ga")),
        check_vma=False,
    )
    return functools.partial(mapped, tables())
```

time: 1360 us -> 132 us (0.10); the launches traced: 1340 us -> 132 us
  waiting for transfers between devices: 784 us -> 0 us
  local copies, waits for them, and re-layouts: 436 us -> 9.39 us
  Pallas kernels: 0 us -> 120 us
  other arithmetic: 43.3 us -> 2.04 us
  matrix products: 38.1 us -> 0 us
  starting transfers between devices: 24.3 us -> 0 us
  between operations: 14.6 us -> 0.66 us
    reduce_scatter x1 -> x0, waiting for transfers between devices: 631 us -> none  [shards(): lax.psum_scatter(blocks, ('band', 'ga'), scatter_dimension=0, tiled=True)[0]]
    unnamed x35 -> x3, local copies, waits for them, and re-layouts: 220 us -> 0.6 us
    psum x1 -> x0, waiting for transfers between devices: 154 us -> none  [shards(): whole_grid = lax.psum(term_grid, ('band', 'ga'))]
    pallas_call x0 -> x1, Pallas kernels: none -> 120 us  [shards(): pl.pallas_call(kernel, out_shape=(jax.ShapeDtypeStruct((2, 8, 4, ROWS, N)...]
    all_to_all x4 -> x0, local copies, waits for them, and re-layouts: 101 us -> none  [the longest x1 46.8 us: shards(): lax.all_to_all(applied_waves, 'band', split_axis=3, concat_axis=1, tiled=...]
    convert_element_type x1 -> x0, local copies, waits for them, and re-layouts: 39.6 us -> none  [shards(): applied_waves = (kinetic * waves_grid.astype(jnp.float32) + recip_part).a...]
    dot_general x6 -> x0, matrix products: 38.1 us -> none  [the longest x1 10.9 us: shards(): jnp.einsum('cnypx,txsk->ctnpsyk', weighted, table_rows.reshape(2, NX, ga_...]
    another operation x6 -> x0, other arithmetic: 35.1 us -> none
  transfers between devices with their start and end apart: 6 -> 0, of which waited for: 2 -> 0; matrix products, arithmetic and copies ran while one was open for 23% -> 0% of each run, Pallas kernels for 0% -> 0%
where the time goes in v1:
time: 132 us
  Pallas kernels  120 us (91%)
  local copies, waits for them, and re-layouts  9.39 us (7%)
  other arithmetic  2.04 us (2%)
    pallas_call x1, Pallas kernels, shards(): pl.pallas_call(kernel, out_shape=(jax.ShapeDtypeStruct((2, 8, 4, ROWS, N)...  120 us
    reshape x1, local copies, waits for them, and re-layouts, shards(): w1 = waves.reshape(2, 8, 4, ROWS, N)  4.54 us
    reshape x1, local copies, waits for them, and re-layouts, shards(): return (out.reshape(2, 8, 4, ROWS * N), sub[:, :, :16])  4.16 us

profile of v1, /device:TPU:1, one launch (start us, length us, event | category | flops | bytes accessed | tf_op | source)
XLA Modules:
  0.0 131.7 jit_solution(7887304929436742045)
XLA Ops:
  0.6 0.1 pad.3.clone
  0.7 0.7 convert_bitcast_fusion
  1.4 1.4 %maximum_maximum_fusion.charges = f32[8,256]{1,0:T(8,128)} fusion(f32[1,256]{1,0:T(1,128)S(1)} %convert_bitcast_fusion, f32[3,256]{1,0:T(4,128)} %param.9, f32[1,256]{1,0:T(1,128)} %bitcast.7, f32[8]{0:T(128)S(1)} %pad.3.clone), kind=kLoop, calls=%fused_computation | loop fusion | flops 6144 | bytes 13344 | tf_op jit(solution)/shard_map/concatenate | solution.py:372
  2.8 4.5 %reshape.24.w1 = bf16[2,8,4,48,384]{4,3,2,1,0:T(8,128)(2,1)} reshape(bf16[2,8,4,18432]{3,2,1,0:T(4,128)(2,1)} %param.6) | data formatting | bytes 4718592 | tf_op jit(solution)/shard_map/reshape | solution.py:371
  7.3 119.7 %shard_map.77 = (bf16[2,8,4,48,384]{4,3,2,1,0:T(8,128)(2,1)}, f32[2,8,128]{2,1,0:T(8,128)}) custom-call(bf16[2,8,4,48,384]{4,3,2,1,0:T(8,128)(2,1)} %reshape.24.w1, f32[8,256]{1,0:T(8,128)} %maximum_maximum_fusion.charges, f32[48,1536]{1,0:T(8,128)} %ionic.1, bf16[2,384,384]{2,1,0:T(8,128)(2,1)} %constant.4.clone.tab), custom_call_target="tpu_custom_call" | custom-call | tf_op jit(solution)/shard_map/pallas_call | solution.py:383
  127.0 0.0 copy-start
  127.0 4.2 %reshape.25 = bf16[2,8,4,18432]{3,2,1,0:T(4,128)(2,1)} reshape(bf16[2,8,4,48,384]{4,3,2,1,0:T(8,128)(2,1)} %get-tuple-element.4) | data formatting | bytes 4718592 | tf_op jit(solution)/shard_map/reshape | solution.py:439
  131.1 0.0 copy-done
  131.1 0.6 copy.9
  (1 shorter events, 0.0 us)
Async XLA Ops:
  127.0 4.2 %copy-start = (f32[2,8,128]{2,1,0:T(8,128)S(1)}, f32[2,8,128]{2,1,0:T(8,128)}, u32[]{:S(2)}) copy-start(f32[2,8,128]{2,1,0:T(8,128)} %get-tuple-element.5) | copy-start | bytes 24580

commit v2 on v1

v2 whole, which is shorter than its diff:
```python
import functools

import jax
import jax.numpy as jnp
import ml_dtypes
import numpy as np
from jax import lax
from jax.experimental import pallas as pl
from jax.experimental.pallas import tpu as pltpu
from jax.sharding import PartitionSpec as P

N = 384
ROWS = 48
BF = jnp.bfloat16
F32 = jnp.float32
MESH = pl.DeviceIdType.MESH


def tables():
    indices = np.arange(N, dtype=np.int32)
    phases = indices[:, None] * indices[None, :] % N
    angles = phases.astype(np.float32) * np.float32(2.0 * np.pi / N)
    factor = np.float32(1.0) / np.sqrt(np.float32(N))
    both = np.stack([np.cos(angles) * factor, np.sin(angles) * factor])
    return both.astype(ml_dtypes.bfloat16).astype(np.float32)


def dot(a, b):
    return jnp.dot(a, b, preferred_element_type=F32)


def dot_nt(a, b):
    return lax.dot_general(a, b, (((1,), (1,)), ((), ())), preferred_element_type=F32)


def split(value):
    high = value.astype(BF)
    return high, (value - high.astype(F32)).astype(BF)


def gaussian(distance):
    return jnp.exp(-distance * distance / 4.5)


SHIFTS = (
    (0, 1), (1, 0), (0, 3), (3, 0), (2, 2), (1, 1), (3, 3), (1, 3),
    (3, 1), (0, 2), (2, 0), (1, 2), (2, 1), (3, 2), (2, 3),
)
PARTS = 4
PART = 12 // PARTS


def each(low, high, body):
    def step(k, c):
        body(k)
        return c

    lax.fori_loop(low, high, step, 0)


def at(start, size, step):
    return pl.ds(pl.multiple_of(start * size, step), size)


def place_of(row):
    m = row >> 4
    plane = (m * 11) >> 5
    return ((row & 15) * 3 + m - 3 * plane) * 4 + plane


def kernel(
    waves, charge, place, slab_in, ionic, tab_in, out, sub,
    xin, w1, tab, spread, m1, m2, perm, kin, zb, w2, xw, phi, wide, ph, p2, xp, ab, fs, ts, bs,
    chs, ch, ios, iop, pot, rsb, own, pf, vyx, vxy, gt, sa, st, sb,
    zi_s, zi_r, zo_s, zo_r, ch_s, ch_r, io_s, io_r, rs_s, rs_r, ag_s, ag_r,
    sp_s, sp_r, sf_s, sf_r, xw_s, xw_r, xp_s, xp_r, sa_s, sa_r, sb_s, sb_r, loc,
):
    b = lax.axis_index("band")
    g = lax.axis_index("ga")
    z = g // 2
    h = lax.rem(g, 2)
    sibling = g + 1 - 2 * h
    b_y = b // 4
    b_x = lax.rem(b, 4)

    def ga_peer(k):
        return lax.rem(g + k, 8)

    def band_peer(k):
        return lax.rem(b + k, 16)

    def shifted(dy, dx):
        return lax.rem(b_y + dy, 4) * 4 + lax.rem(b_x + dx, 4)

    def remote(src, dst, send, recv, band, ga):
        return pltpu.make_async_remote_copy(
            src_ref=src, dst_ref=dst, send_sem=send, recv_sem=recv,
            device_id=(band, ga), device_id_type=MESH,
        )

    barrier = pltpu.get_barrier_semaphore()
    each(1, 8, lambda k: pl.semaphore_signal(
        barrier, inc=1, device_id=(b, ga_peer(k)), device_id_type=MESH))
    each(1, 16, lambda k: pl.semaphore_signal(
        barrier, inc=1, device_id=(band_peer(k), g), device_id_type=MESH))

    def load(n):
        return pltpu.make_async_copy(
            waves.at[:, pl.ds(2 * n, 2)], xin.at[:, pl.ds(2 * n, 2)], loc.at[n]
        )

    def load_tab():
        return pltpu.make_async_copy(tab_in, tab, loc.at[4])

    for n in range(4):
        load(n).start()
    load_tab().start()

    lead = lax.broadcasted_iota(jnp.int32, (192, 192), 0)
    last = lax.broadcasted_iota(jnp.int32, (192, 192), 1)
    spread[...] = jnp.where(last == place_of(lead), 1.0, 0.0).astype(BF)

    def to_planes(n):
        load(n).wait()
        for core in range(2):
            def block(x, core=core):
                both = jnp.concatenate(
                    [xin[c, 2 * n + core, at(x, 12, 12)].reshape(192, 128) for c in range(2)],
                    axis=1,
                )
                rows = dot(spread[...], both).astype(BF)
                for m in range(12):
                    for c in range(2):
                        w1[c, 2 * n + core, m // 3, at(x, 16, 16), m % 3 * 128 : m % 3 * 128 + 128] = (
                            rows[16 * m : 16 * m + 16, 128 * c : 128 * c + 128]
                        )

            each(0, 3, block)

    chs[0:1] = charge[...]
    chs[1:4] = place[...]
    chs[4:5] = slab_in[...].astype(F32)
    chs[5:8] = jnp.zeros((3, 256), F32)
    to_planes(0)
    pl.semaphore_wait(barrier, 22)

    def local(src, dst, sem):
        pltpu.make_async_copy(src, dst, sem).start()

    def await_bytes(like, sem):
        pltpu.make_async_copy(like, like, sem).wait()

    def ch_send(target):
        remote(chs, ch.at[g], ch_s.at[0], ch_r.at[0], b, target).start()

    io_sends = lax.rem(g, 4) == b_y
    io_half = g // 4
    io_source = 4 * h + b_y

    def io_copy(plane):
        return remote(
            ios.at[plane], iop, io_s.at[plane], io_r.at[0], b, 2 * plane + io_half
        )

    def zi_send(n, target):
        remote(
            w1.at[:, 2 * n + lax.rem(target, 2), target // 2],
            zb.at[:, n, at(g, ROWS, 16), :], zi_s.at[0], zi_r.at[n], b, target,
        ).start()

    def zo_send(n, target):
        remote(
            ab.at[:, n, at(target, ROWS, 16), :],
            out.at[:, 2 * n + h, z], zo_s.at[0], zo_r.at[n], b, target,
        ).start()

    def row_sends(q, src, dst, send, recv):
        def to(target):
            return src.at[pl.ds(12 * target + PART * q, PART)], dst.at[pl.ds(PART * q, PART), at(b, 16, 16), :]

        for dy, dx in SHIFTS:
            target = shifted(dy, dx)
            one, other = to(target)
            remote(one, other, send.at[0], recv.at[q], target, g).start()
        one, other = to(b)
        local(one, other, recv.at[q])

    def sp_copy(half):
        return remote(pf.at[half], pf.at[half], sp_s.at[0], sp_r.at[0], b, sibling)

    def sf_copy(n, core):
        return remote(
            phi.at[n, :, at(1 - core, 192, 16), :], ph.at[:, 2 * n + core],
            sf_s.at[0], sf_r.at[n], b, sibling,
        )

    each(1, 8, lambda k: ch_send(ga_peer(k)))
    local(chs, ch.at[g], ch_r.at[0])
    for n in range(4):
        if n:
            to_planes(n)
        each(1, 8, lambda k, n=n: zi_send(n, ga_peer(k)))
        local(w1.at[:, 2 * n + h, z], zb.at[:, n, at(g, ROWS, 16), :], zi_r.at[n])

    to = lax.broadcasted_iota(jnp.int32, (256, 256), 0)
    of = lax.broadcasted_iota(jnp.int32, (256, 256), 1)
    perm[...] = jnp.where(
        ((to >> 4) == (of & 15)) & ((to & 15) == (of >> 4)), 1.0, 0.0
    ).astype(BF)
    for p in range(4):
        def turn(x, p=p):
            block = w1[:, :, p, at(x, 16, 16), :].reshape(256, N)
            turned = dot(perm[...], block).astype(BF).reshape(16, 16, N)
            w2[pl.ds(ROWS * p + 16 * x, 16)] = turned

        each(0, 3, turn)

    def send_waves(q):
        row_sends(q, w2, xw, xw_s, xw_r)

    send_waves(0)

    @pl.when(io_sends)
    def _():
        for j in range(4):
            @pl.when(b_x == j)
            def _(j=j):
                for plane in range(4):
                    rows = ionic[12 * j : 12 * j + 12, plane * N : (plane + 1) * N]
                    ios[plane] = jnp.concatenate([rows, jnp.zeros((4, N), F32)], axis=0)
        for plane in range(4):
            @pl.when(2 * plane + io_half != g)
            def _(plane=plane):
                io_copy(plane).start()

    load_tab().wait()
    c = tab[0].astype(BF)
    s = tab[1].astype(BF)
    m1[0:N, 0:N] = c
    m1[0:N, N : 2 * N] = s
    m1[N : 2 * N, 0:N] = -s
    m1[N : 2 * N, N : 2 * N] = c
    m2[0:N, 0:N] = c
    m2[0:N, N : 2 * N] = -s
    m2[N : 2 * N, 0:N] = s
    m2[N : 2 * N, N : 2 * N] = c

    def frequency(indices):
        return jnp.where(indices < N // 2, indices, indices - N).astype(F32)

    fx = frequency(lax.broadcasted_iota(jnp.int32, (N, N), 0))
    fy = frequency(lax.broadcasted_iota(jnp.int32, (N, N), 1))
    kin[...] = 2.0 * (fx * fx / (N * N) + fy * fy / (N * N))

    await_bytes(ch, ch_r.at[0])
    pot[...] = jnp.zeros((256, N), F32)

    def add_charges(source):
        rows = ch[source]
        q, u, v, w, slab = (rows[i : i + 1] for i in range(5))
        r = lax.broadcasted_iota(jnp.int32, (256, 256), 0)
        y = 192 * h + 12 * (r >> 4) + (r & 15)
        weight = q * gaussian(z.astype(F32) - 4.0 * w)
        inside = ((y * 1366) >> 16).astype(F32) == slab
        gy = gaussian(y.astype(F32) - (slab * 48.0 + 48.0 * v)) * weight
        gy = jnp.where(inside, gy, 0.0)
        x = lax.broadcasted_iota(jnp.int32, (N, 256), 0).astype(F32)
        gx = gaussian(x - 384.0 * u)
        yh, yl = split(gy)
        xh, xl = split(gx)
        pot[...] += dot_nt(yh, xh) + (dot_nt(yh, xl) + dot_nt(yl, xh))

    each(0, 8, add_charges)

    def rs_send(target):
        remote(
            pot.at[at(target, 16, 8), :], rsb.at[b], rs_s.at[0], rs_r.at[0], target, g
        ).start()

    each(1, 16, lambda k: rs_send(band_peer(k)))
    local(pot.at[at(b, 16, 8), :], rsb.at[b], rs_r.at[0])
    for q in range(1, PARTS):
        send_waves(q)

    def forward(n):
        await_bytes(zb.at[:, n], zi_r.at[n])
        both = jnp.concatenate([zb[0, n], zb[1, n]], axis=1)
        fs[0:N] = dot(both, m1[:, 0:N]).astype(BF)
        fs[N : 2 * N] = dot(both, m1[:, N : 2 * N]).astype(BF)
        for part in range(2):
            space = dot(m2[part * N : (part + 1) * N], fs[...])
            wide[n, part] = space
            phi[n, part] = space.astype(BF)
        sf_copy(n, h).start()
        for part in range(2):
            ph[part, 2 * n + h] = phi[n, part, at(h, 192, 16), :]

    forward(0)

    await_bytes(rsb, rs_r.at[0])

    @pl.when(io_source == g)
    def _():
        iop[...] = ios[z]

    @pl.when(io_source != g)
    def _():
        io_copy(z).wait_recv()

    piece = iop[...]
    for k in range(16):
        piece = piece + rsb[k]
    own[...] = piece.astype(BF)

    def ag_send(target):
        remote(own, pf.at[h, at(b, 16, 16), :], ag_s.at[0], ag_r.at[0], target, g).start()

    each(1, 16, lambda k: ag_send(band_peer(k)))
    local(own, pf.at[h, at(b, 16, 16), :], ag_r.at[0])
    each(1, 4, forward)
    await_bytes(pf.at[h], ag_r.at[0])
    sp_copy(h).start()

    each(0, 4, lambda n: sf_copy(n, 1 - h).wait_recv())

    def turn_field(x):
        block = ph[:, :, at(x, 16, 16), :].reshape(256, N)
        p2[at(x, 16, 16)] = dot(perm[...], block).astype(BF).reshape(16, 16, N)

    each(0, 12, turn_field)
    for q in range(PARTS):
        row_sends(q, p2, xp, xp_s, xp_r)

    sp_copy(1 - h).wait_recv()
    for half in range(2):
        def join(q, half=half):
            two = pf[half, at(q, 32, 16), :].astype(F32)
            dst = pl.ds(pl.multiple_of(192 * half + 24 * q, 8), 24)
            vyx[dst, :] = jnp.concatenate([two[0:12], two[16:28]], axis=0)

        each(0, 8, join)
    vxy[...] = vyx[...].T

    def backward(n):
        for part in range(2):
            ts[part * N : (part + 1) * N] = (wide[n, part] * vxy[...]).astype(BF)
        for part in range(2):
            bs[:, part * N : (part + 1) * N] = dot(
                m1[part * N : (part + 1) * N], ts[...]
            ).astype(BF)
        for part in range(2):
            recip = dot(bs[...], m2[:, part * N : (part + 1) * N])
            ab[part, n] = (kin[...] * zb[part, n].astype(F32) + recip).astype(BF)
        each(1, 8, lambda k: zo_send(n, ga_peer(k)))
        local(ab.at[:, n, at(g, ROWS, 16), :], out.at[:, 2 * n + h, z], zo_r.at[n])

    each(0, 4, backward)

    def gram(data, q, weights):
        rows = [data[PART * q + i] for i in range(PART)]
        scaled = [(r.astype(F32) * w).astype(BF) for r, w in zip(rows, weights)]
        gt[...] += dot_nt(jnp.concatenate(scaled, axis=1), jnp.concatenate(rows, axis=1))

    gt[...] = jnp.zeros((256, 256), F32)

    def gram_waves(q):
        await_bytes(xw.at[pl.ds(PART * q, PART)], xw_r.at[q])
        x = [ROWS * g + lax.rem(12 * b + PART * q + i, ROWS) for i in range(PART)]
        gram(xw, q, [kin[pl.ds(i, 1), :] for i in x])

    each(0, PARTS, gram_waves)

    await_bytes(w1.at[:, pl.ds(0, 7)], zi_s.at[0])
    await_bytes(ph.at[:, pl.ds(0, 4)], sf_s.at[0])
    await_bytes(ch.at[pl.ds(0, 7)], ch_s.at[0])
    await_bytes(rsb.at[pl.ds(0, 15)], rs_s.at[0])
    await_bytes(pf.at[0, pl.ds(0, 240)], ag_s.at[0])
    await_bytes(w2.at[pl.ds(0, 180)], xw_s.at[0])
    sp_copy(h).wait_send()

    @pl.when(io_sends)
    def _():
        for plane in range(4):
            @pl.when(2 * plane + io_half != g)
            def _(plane=plane):
                io_copy(plane).wait_send()

    def finish(n):
        await_bytes(out.at[:, pl.ds(2 * n, 2)], zo_r.at[n])

    def gram_fields(q):
        await_bytes(xp.at[pl.ds(PART * q, PART)], xp_r.at[q])
        x = [192 * h + 12 * b + PART * q + i for i in range(PART)]
        gram(xp, q, [vxy[pl.ds(i, 1), :] for i in x])

    gram_fields(0)
    gram_fields(1)
    gram_fields(2)
    gram_fields(3)

    def sa_send(target):
        remote(
            gt.at[at(target, 32, 8), :], sa.at[g], sa_s.at[0], sa_r.at[0], b, target
        ).start()

    each(1, 8, lambda k: sa_send(ga_peer(k)))
    local(gt.at[at(g, 32, 8), :], sa.at[g], sa_r.at[0])
    await_bytes(p2.at[pl.ds(0, 180)], xp_s.at[0])
    finish(0)
    finish(1)
    await_bytes(sa, sa_r.at[0])
    total = sa[0]
    for k in range(1, 8):
        total = total + sa[k]
    st[...] = jnp.concatenate([total, jnp.zeros((96, 256), F32)], axis=0).T

    def sb_send(target):
        remote(
            st.at[at(target, 16, 8), :], sb.at[b], sb_s.at[0], sb_r.at[0], target, g
        ).start()

    each(1, 16, lambda k: sb_send(band_peer(k)))
    local(st.at[at(b, 16, 8), :], sb.at[b], sb_r.at[0])
    finish(2)
    finish(3)
    await_bytes(w1.at[:, pl.ds(0, 7)], zo_s.at[0])
    await_bytes(sa.at[pl.ds(0, 7)], sa_s.at[0])
    await_bytes(sb, sb_r.at[0])
    block = sb[0]
    for k in range(1, 16):
        block = block + sb[k]
    row = lax.broadcasted_iota(jnp.int32, (128, 128), 0)
    col = lax.broadcasted_iota(jnp.int32, (128, 128), 1)
    lane = ((col >> 3) << 4) + (col & 7)
    valid = col < 16
    pick_re = jnp.where(valid & (row == lane), 1.0, 0.0)
    pick_im = jnp.where(valid & (row == lane + 8), 1.0, 0.0)

    def pick(rows, which):
        return jnp.dot(rows, which, precision=lax.Precision.HIGHEST, preferred_element_type=F32)

    inverse_cells = 1.0 / (4 * N * N)
    rr, ri = pick(block, pick_re), pick(block, pick_im)
    sub[0] = ((rr[0:8] + ri[8:16]) * inverse_cells)[:, 0:16]
    sub[1] = ((ri[0:8] - rr[8:16]) * inverse_cells)[:, 0:16]

    await_bytes(sb.at[pl.ds(0, 15)], sb_s.at[0])


def shards(table, waves, ionic_field, point_charge, charge_place, charge_slab):
    tiled = waves.reshape(2, 8, 4, 144, 128).transpose(0, 1, 3, 2, 4).reshape(2, 8, 36, 16, 128)
    dma = pltpu.SemaphoreType.DMA
    vmem = pltpu.VMEM
    hbm = pl.BlockSpec(memory_space=pltpu.MemorySpace.HBM)
    out, sub = pl.pallas_call(
        kernel,
        out_shape=(
            jax.ShapeDtypeStruct((2, 8, 4, ROWS, N), BF),
            jax.ShapeDtypeStruct((2, 8, 16), F32),
        ),
        in_specs=[hbm] + [pl.BlockSpec(memory_space=pltpu.VMEM)] * 4 + [hbm],
        out_specs=(
            hbm,
            pl.BlockSpec(memory_space=pltpu.VMEM),
        ),
        scratch_shapes=[
            vmem((2, 8, 36, 16, 128), BF),
            vmem((2, 8, 4, ROWS, N), BF),
            vmem((2, N, N), F32),
            vmem((192, 192), BF),
            vmem((2 * N, 2 * N), BF),
            vmem((2 * N, 2 * N), BF),
            vmem((256, 256), BF),
            vmem((N, N), F32),
            vmem((2, 4, N, N), BF),
            vmem((192, 16, N), BF),
            vmem((12, 256, N), BF),
            vmem((4, 2, N, N), BF),
            vmem((4, 2, N, N), F32),
            vmem((2, 8, 192, N), BF),
            vmem((192, 16, N), BF),
            vmem((12, 256, N), BF),
            vmem((2, 4, N, N), BF),
            vmem((2 * N, N), BF),
            vmem((2 * N, N), BF),
            vmem((N, 2 * N), BF),
            vmem((8, 256), F32),
            vmem((8, 8, 256), F32),
            vmem((4, 16, N), F32),
            vmem((16, N), F32),
            vmem((256, N), F32),
            vmem((16, 16, N), F32),
            vmem((16, N), BF),
            vmem((2, 256, N), BF),
            vmem((N, N), F32),
            vmem((N, N), F32),
            vmem((256, 256), F32),
            vmem((8, 32, 256), F32),
            vmem((256, 128), F32),
            vmem((16, 16, 128), F32),
            dma((1,)), dma((4,)),
            dma((1,)), dma((4,)),
            dma((1,)), dma((1,)),
            dma((4,)), dma((1,)),
            dma((1,)), dma((1,)),
            dma((1,)), dma((1,)),
            dma((1,)), dma((1,)),
            dma((1,)), dma((4,)),
            dma((1,)), dma((PARTS,)),
            dma((1,)), dma((PARTS,)),
            dma((1,)), dma((1,)),
            dma((1,)), dma((1,)),
            dma((5,)),
        ],
        compiler_params=pltpu.CompilerParams(
            collective_id=0, has_side_effects=True, vmem_limit_bytes=56 * 1024 * 1024
        ),
    )(
        tiled, point_charge.reshape(1, 256), charge_place, charge_slab.reshape(1, 256),
        ionic_field, table,
    )
    return out.reshape(2, 8, 4, ROWS * N), sub


def solution(mesh):
    placed = (
        P(None, "band", None, "ga"),
        P("ga", None),
        P(("band", "ga")),
        P(None, ("band", "ga")),
        P(("band", "ga"), None),
    )
    mapped = jax.shard_map(
        shards,
        mesh=mesh,
        in_specs=(P(None, None, None),) + placed,
        out_specs=(P(None, "band", None, "ga"), P(None, "band", "ga")),
        check_vma=False,
    )
    return functools.partial(mapped, tables())
```

time: 132 us -> 97.3 us (0.74)
  Pallas kernels: 120 us -> 91.7 us
  local copies, waits for them, and re-layouts: 9.39 us -> 4.76 us
  other arithmetic: 2.04 us -> 0 us
    pallas_call x1, Pallas kernels: 120 us -> 91.7 us  [shards(): pl.pallas_call(kernel, out_shape=(jax.ShapeDtypeStruct((2, 8, 4, ROWS, N)...]
    reshape x2 -> x1, local copies, waits for them, and re-layouts: 8.71 us -> 4.16 us  [shards(): return (out.reshape(2, 8, 4, ROWS * N), sub)]
    concatenate x1 -> x0, other arithmetic: 1.36 us -> none  [shards(): jnp.concatenate([point_charge[None, :], charge_place, charge_slab.reshape...]
where the time goes in v2:
time: 97.3 us; the launch traced here: 97.1 us
  Pallas kernels  91.7 us (94%)
  local copies, waits for them, and re-layouts  4.76 us (5%)
    pallas_call x1, Pallas kernels, shards(): pl.pallas_call(kernel, out_shape=(jax.ShapeDtypeStruct((2, 8, 4, ROWS, N)...  91.7 us
    reshape x1, local copies, waits for them, and re-layouts, shards(): return (out.reshape(2, 8, 4, ROWS * N), sub)  4.16 us

profile of v2, /device:TPU:1, one launch (start us, length us, event | category | flops | bytes accessed | tf_op | source)
XLA Modules:
  0.0 97.1 jit_solution(4075386484626040223)
XLA Ops:
  0.6 91.7 %shard_map.77 = (bf16[2,8,4,48,384]{4,3,2,1,0:T(8,128)(2,1)}, f32[2,8,16]{2,1,0:T(8,128)}) custom-call(bf16[2,8,36,16,128]{4,3,2,1,0:T(8,128)(2,1)} %bitcast.9, f32[1,256]{1,0:T(1,128)} %bitcast.10, f32[3,256]{1,0:T(4,128)} %place.1, s32[1,256]{1,0:T(1,128)} %bitcast.11, f32[48,1536]{1,0:T(8,128)} %ionic.1, f32[2,384,384]{2,1,0:T(8,128)} %constant.2.clone.tab_in), custom_call_target="tpu_custom_call" | custom-call | tf_op jit(solution)/shard_map/pallas_call | solution.py:455
  92.4 0.0 copy-start
  92.4 4.2 %reshape.23 = bf16[2,8,4,18432]{3,2,1,0:T(4,128)(2,1)} reshape(bf16[2,8,4,48,384]{4,3,2,1,0:T(8,128)(2,1)} %get-tuple-element.4) | data formatting | bytes 4718592 | tf_op jit(solution)/shard_map/reshape | solution.py:522
  96.5 0.0 copy-done
  96.5 0.6 copy.10
Async XLA Ops:
  92.4 4.2 %copy-start = (f32[2,8,16]{2,1,0:T(8,128)S(1)}, f32[2,8,16]{2,1,0:T(8,128)}, u32[]{:S(2)}) copy-start(f32[2,8,16]{2,1,0:T(8,128)} %get-tuple-element.9) | copy-start | bytes 3076

commit v3 on v2

--- a/solution.py
+++ b/solution.py
@@ -70,10 +70,10 @@
 
 def kernel(
     waves, charge, place, slab_in, ionic, tab_in, out, sub,
-    xin, w1, tab, spread, m1, m2, perm, kin, zb, w2, xw, phi, wide, ph, p2, xp, ab, fs, ts, bs,
-    chs, ch, ios, iop, pot, rsb, own, pf, vyx, vxy, gt, sa, st, sb,
+    xin, w1, tab, rows_in, xout, spread, gather, m1, m2, perm, kin, zb, w2, xw, phi, wide, ph, p2, xp, ab, fs, ts, bs,
+    chs, ch, ios, iop, pot, rsb, own, pf, vyx, vxy, gt, gb, sa, st, sb,
     zi_s, zi_r, zo_s, zo_r, ch_s, ch_r, io_s, io_r, rs_s, rs_r, ag_s, ag_r,
-    sp_s, sp_r, sf_s, sf_r, xw_s, xw_r, xp_s, xp_r, sa_s, sa_r, sb_s, sb_r, loc,
+    sp_s, sp_r, sf_s, sf_r, xw_s, xw_r, xp_s, xp_r, sa_s, sa_r, sb_s, sb_r, loc, st_s,
 ):
     b = lax.axis_index("band")
     g = lax.axis_index("ga")
@@ -119,29 +119,67 @@
     lead = lax.broadcasted_iota(jnp.int32, (192, 192), 0)
     last = lax.broadcasted_iota(jnp.int32, (192, 192), 1)
     spread[...] = jnp.where(last == place_of(lead), 1.0, 0.0).astype(BF)
+    gather[...] = jnp.where(lead == place_of(last), 1.0, 0.0).astype(BF)
 
     def to_planes(n):
         load(n).wait()
         for core in range(2):
-            def block(x, core=core):
+            for x in range(3):
                 both = jnp.concatenate(
-                    [xin[c, 2 * n + core, at(x, 12, 12)].reshape(192, 128) for c in range(2)],
+                    [xin[c, 2 * n + core, 12 * x : 12 * x + 12].reshape(192, 128) for c in range(2)],
                     axis=1,
                 )
                 rows = dot(spread[...], both).astype(BF)
                 for m in range(12):
+                    part = m % 3 * 128
                     for c in range(2):
-                        w1[c, 2 * n + core, m // 3, at(x, 16, 16), m % 3 * 128 : m % 3 * 128 + 128] = (
+                        w1[c, 2 * n + core, m // 3, 16 * x : 16 * x + 16, part : part + 128] = (
                             rows[16 * m : 16 * m + 16, 128 * c : 128 * c + 128]
                         )
 
-            each(0, 3, block)
+    def from_planes(n):
+        for core in range(2):
+            for x in range(3):
+                both = jnp.concatenate(
+                    [
+                        jnp.concatenate(
+                            [
+                                rows_in[
+                                    c, 2 * n + core, m // 3, 16 * x : 16 * x + 16,
+                                    m % 3 * 128 : m % 3 * 128 + 128,
+                                ]
+                                for m in range(12)
+                            ],
+                            axis=0,
+                        )
+                        for c in range(2)
+                    ],
+                    axis=1,
+                )
+                rows = dot(gather[...], both).astype(BF)
+                for c in range(2):
+                    xout[c, 2 * n + core, 12 * x : 12 * x + 12] = rows[
+                        :, 128 * c : 128 * c + 128
+                    ].reshape(12, 16, 128)
 
     chs[0:1] = charge[...]
     chs[1:4] = place[...]
     chs[4:5] = slab_in[...].astype(F32)
     chs[5:8] = jnp.zeros((3, 256), F32)
-    to_planes(0)
+    each(0, 4, to_planes)
+
+    to = lax.broadcasted_iota(jnp.int32, (256, 256), 0)
+    of = lax.broadcasted_iota(jnp.int32, (256, 256), 1)
+    perm[...] = jnp.where(
+        ((to >> 4) == (of & 15)) & ((to & 15) == (of >> 4)), 1.0, 0.0
+    ).astype(BF)
+    def turn(p):
+        for x in range(3):
+            block = w1[:, :, p, 16 * x : 16 * x + 16, :].reshape(256, N)
+            turned = dot(perm[...], block).astype(BF).reshape(16, 16, N)
+            w2[pl.ds(ROWS * p + 16 * x, 16)] = turned
+
+    each(0, 4, turn)
     pl.semaphore_wait(barrier, 22)
 
     def local(src, dst, sem):
@@ -171,7 +209,7 @@
     def zo_send(n, target):
         remote(
             ab.at[:, n, at(target, ROWS, 16), :],
-            out.at[:, 2 * n + h, z], zo_s.at[0], zo_r.at[n], b, target,
+            rows_in.at[:, 2 * n + h, z], zo_s.at[0], zo_r.at[n], b, target,
         ).start()
 
     def row_sends(q, src, dst, send, recv):
@@ -196,29 +234,18 @@
 
     each(1, 8, lambda k: ch_send(ga_peer(k)))
     local(chs, ch.at[g], ch_r.at[0])
-    for n in range(4):
-        if n:
-            to_planes(n)
-        each(1, 8, lambda k, n=n: zi_send(n, ga_peer(k)))
+    def zi_all(n):
+        each(1, 8, lambda k: zi_send(n, ga_peer(k)))
         local(w1.at[:, 2 * n + h, z], zb.at[:, n, at(g, ROWS, 16), :], zi_r.at[n])
 
-    to = lax.broadcasted_iota(jnp.int32, (256, 256), 0)
-    of = lax.broadcasted_iota(jnp.int32, (256, 256), 1)
-    perm[...] = jnp.where(
-        ((to >> 4) == (of & 15)) & ((to & 15) == (of >> 4)), 1.0, 0.0
-    ).astype(BF)
-    for p in range(4):
-        def turn(x, p=p):
-            block = w1[:, :, p, at(x, 16, 16), :].reshape(256, N)
-            turned = dot(perm[...], block).astype(BF).reshape(16, 16, N)
-            w2[pl.ds(ROWS * p + 16 * x, 16)] = turned
-
-        each(0, 3, turn)
+    zi_all(0)
 
     def send_waves(q):
         row_sends(q, w2, xw, xw_s, xw_r)
 
     send_waves(0)
+    send_waves(1)
+    each(1, 4, zi_all)
 
     @pl.when(io_sends)
     def _():
@@ -270,7 +297,11 @@
         xh, xl = split(gx)
         pot[...] += dot_nt(yh, xh) + (dot_nt(yh, xl) + dot_nt(yl, xh))
 
-    each(0, 8, add_charges)
+    def add_two(i):
+        add_charges(2 * i)
+        add_charges(2 * i + 1)
+
+    each(0, 4, add_two)
 
     def rs_send(target):
         remote(
@@ -279,8 +310,7 @@
 
     each(1, 16, lambda k: rs_send(band_peer(k)))
     local(pot.at[at(b, 16, 8), :], rsb.at[b], rs_r.at[0])
-    for q in range(1, PARTS):
-        send_waves(q)
+    send_waves(2)
 
     def forward(n):
         await_bytes(zb.at[:, n], zi_r.at[n])
@@ -295,7 +325,7 @@
         for part in range(2):
             ph[part, 2 * n + h] = phi[n, part, at(h, 192, 16), :]
 
-    forward(0)
+    each(0, 2, forward)
 
     await_bytes(rsb, rs_r.at[0])
 
@@ -317,17 +347,19 @@
 
     each(1, 16, lambda k: ag_send(band_peer(k)))
     local(own, pf.at[h, at(b, 16, 16), :], ag_r.at[0])
-    each(1, 4, forward)
+    send_waves(3)
+    each(2, 4, forward)
     await_bytes(pf.at[h], ag_r.at[0])
     sp_copy(h).start()
 
     each(0, 4, lambda n: sf_copy(n, 1 - h).wait_recv())
 
-    def turn_field(x):
-        block = ph[:, :, at(x, 16, 16), :].reshape(256, N)
-        p2[at(x, 16, 16)] = dot(perm[...], block).astype(BF).reshape(16, 16, N)
-
-    each(0, 12, turn_field)
+    def turn_field(p):
+        for x in range(3):
+            block = ph[:, :, at(3 * p + x, 16, 16), :].reshape(256, N)
+            p2[at(3 * p + x, 16, 16)] = dot(perm[...], block).astype(BF).reshape(16, 16, N)
+
+    each(0, 4, turn_field)
     for q in range(PARTS):
         row_sends(q, p2, xp, xp_s, xp_r)
 
@@ -352,14 +384,14 @@
             recip = dot(bs[...], m2[:, part * N : (part + 1) * N])
             ab[part, n] = (kin[...] * zb[part, n].astype(F32) + recip).astype(BF)
         each(1, 8, lambda k: zo_send(n, ga_peer(k)))
-        local(ab.at[:, n, at(g, ROWS, 16), :], out.at[:, 2 * n + h, z], zo_r.at[n])
+        local(ab.at[:, n, at(g, ROWS, 16), :], rows_in.at[:, 2 * n + h, z], zo_r.at[n])
 
     each(0, 4, backward)
 
     def gram(data, q, weights):
         rows = [data[PART * q + i] for i in range(PART)]
         scaled = [(r.astype(F32) * w).astype(BF) for r, w in zip(rows, weights)]
-        gt[...] += dot_nt(jnp.concatenate(scaled, axis=1), jnp.concatenate(rows, axis=1))
+        gt[...] += dot_nt(jnp.concatenate(rows, axis=1), jnp.concatenate(scaled, axis=1))
 
     gt[...] = jnp.zeros((256, 256), F32)
 
@@ -386,7 +418,13 @@
                 io_copy(plane).wait_send()
 
     def finish(n):
-        await_bytes(out.at[:, pl.ds(2 * n, 2)], zo_r.at[n])
+        await_bytes(rows_in.at[:, pl.ds(2 * n, 2)], zo_r.at[n])
+        from_planes(n)
+        store(n).start()
+
+    def store(n):
+        bands = pl.ds(2 * n, 2)
+        return pltpu.make_async_copy(xout.at[:, bands], out.at[:, bands], st_s.at[n])
 
     def gram_fields(q):
         await_bytes(xp.at[pl.ds(PART * q, PART)], xp_r.at[q])
@@ -398,37 +436,38 @@
     gram_fields(2)
     gram_fields(3)
 
+    gb[...] = gt[...].astype(BF)
+
+    def sb_send(target):
+        remote(
+            gb.at[at(target, 16, 16), :], sb.at[b], sb_s.at[0], sb_r.at[0], target, g
+        ).start()
+
+    each(1, 16, lambda k: sb_send(band_peer(k)))
+    local(gb.at[at(b, 16, 16), :], sb.at[b], sb_r.at[0])
+    await_bytes(p2.at[pl.ds(0, 180)], xp_s.at[0])
+    each(0, 2, finish)
+    await_bytes(sb, sb_r.at[0])
+    total = sb[0].astype(F32)
+    for k in range(1, 16):
+        total = total + sb[k].astype(F32)
+    st[...] = jnp.concatenate([total, jnp.zeros((112, 256), F32)], axis=0).T
+
     def sa_send(target):
         remote(
-            gt.at[at(target, 32, 8), :], sa.at[g], sa_s.at[0], sa_r.at[0], b, target
+            st.at[at(target, 32, 8), :], sa.at[g], sa_s.at[0], sa_r.at[0], b, target
         ).start()
 
     each(1, 8, lambda k: sa_send(ga_peer(k)))
-    local(gt.at[at(g, 32, 8), :], sa.at[g], sa_r.at[0])
-    await_bytes(p2.at[pl.ds(0, 180)], xp_s.at[0])
-    finish(0)
-    finish(1)
+    local(st.at[at(g, 32, 8), :], sa.at[g], sa_r.at[0])
+    each(2, 4, finish)
+    await_bytes(w1.at[:, pl.ds(0, 7)], zo_s.at[0])
+    await_bytes(sb.at[pl.ds(0, 15)], sb_s.at[0])
     await_bytes(sa, sa_r.at[0])
-    total = sa[0]
+    block = sa[0]
     for k in range(1, 8):
-        total = total + sa[k]
-    st[...] = jnp.concatenate([total, jnp.zeros((96, 256), F32)], axis=0).T
-
-    def sb_send(target):
-        remote(
-            st.at[at(target, 16, 8), :], sb.at[b], sb_s.at[0], sb_r.at[0], target, g
-        ).start()
-
-    each(1, 16, lambda k: sb_send(band_peer(k)))
-    local(st.at[at(b, 16, 8), :], sb.at[b], sb_r.at[0])
-    finish(2)
-    finish(3)
-    await_bytes(w1.at[:, pl.ds(0, 7)], zo_s.at[0])
-    await_bytes(sa.at[pl.ds(0, 7)], sa_s.at[0])
-    await_bytes(sb, sb_r.at[0])
-    block = sb[0]
-    for k in range(1, 16):
-        block = block + sb[k]
+        block = block + sa[k]
+    block = jnp.concatenate([block, jnp.zeros((96, 128), F32)], axis=0).T[0:16]
     row = lax.broadcasted_iota(jnp.int32, (128, 128), 0)
     col = lax.broadcasted_iota(jnp.int32, (128, 128), 1)
     lane = ((col >> 3) << 4) + (col & 7)
@@ -444,7 +483,13 @@
     sub[0] = ((rr[0:8] + ri[8:16]) * inverse_cells)[:, 0:16]
     sub[1] = ((ri[0:8] - rr[8:16]) * inverse_cells)[:, 0:16]
 
-    await_bytes(sb.at[pl.ds(0, 15)], sb_s.at[0])
+    await_bytes(sa.at[pl.ds(0, 7)], sa_s.at[0])
+    each(0, 4, lambda n: store(n).wait())
+
+
+def finished(rows, sums, out, sub):
+    out[...] = rows[...]
+    sub[...] = sums[...]
 
 
 def shards(table, waves, ionic_field, point_charge, charge_place, charge_slab):
@@ -455,7 +500,7 @@
     out, sub = pl.pallas_call(
         kernel,
         out_shape=(
-            jax.ShapeDtypeStruct((2, 8, 4, ROWS, N), BF),
+            jax.ShapeDtypeStruct((2, 8, 36, 16, 128), BF),
             jax.ShapeDtypeStruct((2, 8, 16), F32),
         ),
         in_specs=[hbm] + [pl.BlockSpec(memory_space=pltpu.VMEM)] * 4 + [hbm],
@@ -467,6 +512,9 @@
             vmem((2, 8, 36, 16, 128), BF),
             vmem((2, 8, 4, ROWS, N), BF),
             vmem((2, N, N), F32),
+            vmem((2, 8, 4, ROWS, N), BF),
+            vmem((2, 8, 36, 16, 128), BF),
+            vmem((192, 192), BF),
             vmem((192, 192), BF),
             vmem((2 * N, 2 * N), BF),
             vmem((2 * N, 2 * N), BF),
@@ -495,9 +543,10 @@
             vmem((N, N), F32),
             vmem((N, N), F32),
             vmem((256, 256), F32),
-            vmem((8, 32, 256), F32),
+            vmem((256, 256), BF),
+            vmem((8, 32, 128), F32),
             vmem((256, 128), F32),
-            vmem((16, 16, 128), F32),
+            vmem((16, 16, 256), BF),
             dma((1,)), dma((4,)),
             dma((1,)), dma((4,)),
             dma((1,)), dma((1,)),
@@ -511,6 +560,7 @@
             dma((1,)), dma((1,)),
             dma((1,)), dma((1,)),
             dma((5,)),
+            dma((4,)),
         ],
         compiler_params=pltpu.CompilerParams(
             collective_id=0, has_side_effects=True, vmem_limit_bytes=56 * 1024 * 1024
@@ -519,6 +569,19 @@
         tiled, point_charge.reshape(1, 256), charge_place, charge_slab.reshape(1, 256),
         ionic_field, table,
     )
+    halves = pl.BlockSpec((2, 4, 36, 16, 128), lambda i: (0, i, 0, 0, 0))
+    every = pl.BlockSpec((2, 8, 16), lambda i: (0, 0, 0))
+    out, sub = pl.pallas_call(
+        finished,
+        out_shape=(
+            jax.ShapeDtypeStruct((2, 8, 36, 16, 128), BF),
+            jax.ShapeDtypeStruct((2, 8, 16), F32),
+        ),
+        grid=(2,),
+        in_specs=[halves, every],
+        out_specs=(halves, every),
+    )(out, sub)
+    out = out.reshape(2, 8, 144, 4, 128).transpose(0, 1, 3, 2, 4)
     return out.reshape(2, 8, 4, ROWS * N), sub
 
 

time: 97.3 us -> 88.3 us (0.908)
  local copies, waits for them, and re-layouts: 4.76 us -> 0 us
  Pallas kernels: 91.7 us -> 87.5 us
    pallas_call x1 -> x2, Pallas kernels: 91.7 us -> 87.5 us  [the longest x1 84.7 us: shards(): pl.pallas_call(kernel, out_shape=(jax.ShapeDtypeStruct((2, 8, 36, 16, 128...]
    reshape x1 -> x0, local copies, waits for them, and re-layouts: 4.16 us -> none  [shards(): return (out.reshape(2, 8, 4, ROWS * N), sub)]
where the time goes in v3:
time: 88.3 us; the launch traced here: 88.1 us
  Pallas kernels  87.5 us (99%)
    pallas_call x1, Pallas kernels, shards(): pl.pallas_call(kernel, out_shape=(jax.ShapeDtypeStruct((2, 8, 36, 16, 128...  84.7 us
    pallas_call x1, Pallas kernels, shards(): pl.pallas_call(finished, out_shape=(jax.ShapeDtypeStruct((2, 8, 36, 16, 1...  2.77 us

profile of v3, /device:TPU:1, one launch (start us, length us, event | category | flops | bytes accessed | tf_op | source)
XLA Modules:
  0.0 88.1 jit_solution(7937415564481095793)
XLA Ops:
  0.6 84.7 %shard_map.77 = (bf16[2,8,36,16,128]{4,3,2,1,0:T(8,128)(2,1)}, f32[2,8,16]{2,1,0:T(8,128)}) custom-call(bf16[2,8,36,16,128]{4,3,2,1,0:T(8,128)(2,1)} %bitcast.12, f32[1,256]{1,0:T(1,128)} %bitcast.13, f32[3,256]{1,0:T(4,128)} %place.1, s32[1,256]{1,0:T(1,128)} %bitcast.14, f32[48,1536]{1,0:T(8,128)} %ionic.1, f32[2,384,384]{2,1,0:T(8,128)} %constant.2.clone.tab_in), custom_call_target="tpu_custom_call" | custom-call | tf_op jit(solution)/shard_map/pallas_call | solution.py:500
  85.3 2.8 %shard_map.78 = (bf16[2,8,36,16,128]{4,3,2,1,0:T(8,128)(2,1)}, f32[2,8,16]{2,1,0:T(8,128)}) custom-call(bf16[2,8,36,16,128]{4,3,2,1,0:T(8,128)(2,1)} %get-tuple-element.6.rows, f32[2,8,16]{2,1,0:T(8,128)} %get-tuple-element.7.sums), custom_call_target="tpu_custom_call" | custom-call | tf_op jit(solution)/shard_map/pallas_call | solution.py:574

commit v4 on v3

--- a/solution.py
+++ b/solution.py
@@ -70,10 +70,10 @@
 
 def kernel(
     waves, charge, place, slab_in, ionic, tab_in, out, sub,
-    xin, w1, tab, rows_in, xout, spread, gather, m1, m2, perm, kin, zb, w2, xw, phi, wide, ph, p2, xp, ab, fs, ts, bs,
+    xin, w1, tab, rows_in, spread, gather, m1, m2, perm, kin, zb, w2, xw, phi, wide, ph, p2, xp, ab, fs, ts, bs,
     chs, ch, ios, iop, pot, rsb, own, pf, vyx, vxy, gt, gb, sa, st, sb,
     zi_s, zi_r, zo_s, zo_r, ch_s, ch_r, io_s, io_r, rs_s, rs_r, ag_s, ag_r,
-    sp_s, sp_r, sf_s, sf_r, xw_s, xw_r, xp_s, xp_r, sa_s, sa_r, sb_s, sb_r, loc, st_s,
+    sp_s, sp_r, sf_s, sf_r, xw_s, xw_r, xp_s, xp_r, sa_s, sa_r, sb_s, sb_r, loc,
 ):
     b = lax.axis_index("band")
     g = lax.axis_index("ga")
@@ -158,7 +158,7 @@
                 )
                 rows = dot(gather[...], both).astype(BF)
                 for c in range(2):
-                    xout[c, 2 * n + core, 12 * x : 12 * x + 12] = rows[
+                    out[c, 2 * n + core, 12 * x : 12 * x + 12] = rows[
                         :, 128 * c : 128 * c + 128
                     ].reshape(12, 16, 128)
 
@@ -214,7 +214,7 @@
 
     def row_sends(q, src, dst, send, recv):
         def to(target):
-            return src.at[pl.ds(12 * target + PART * q, PART)], dst.at[pl.ds(PART * q, PART), at(b, 16, 16), :]
+            return src.at[pl.ds(ROWS * q + PART * target, PART)], dst.at[pl.ds(PART * q, PART), at(b, 16, 16), :]
 
         for dy, dx in SHIFTS:
             target = shifted(dy, dx)
@@ -359,8 +359,8 @@
             block = ph[:, :, at(3 * p + x, 16, 16), :].reshape(256, N)
             p2[at(3 * p + x, 16, 16)] = dot(perm[...], block).astype(BF).reshape(16, 16, N)
 
-    each(0, 4, turn_field)
     for q in range(PARTS):
+        turn_field(q)
         row_sends(q, p2, xp, xp_s, xp_r)
 
     sp_copy(1 - h).wait_recv()
@@ -397,7 +397,7 @@
 
     def gram_waves(q):
         await_bytes(xw.at[pl.ds(PART * q, PART)], xw_r.at[q])
-        x = [ROWS * g + lax.rem(12 * b + PART * q + i, ROWS) for i in range(PART)]
+        x = [ROWS * g + PART * b + i for i in range(PART)]
         gram(xw, q, [kin[pl.ds(i, 1), :] for i in x])
 
     each(0, PARTS, gram_waves)
@@ -420,20 +420,16 @@
     def finish(n):
         await_bytes(rows_in.at[:, pl.ds(2 * n, 2)], zo_r.at[n])
         from_planes(n)
-        store(n).start()
-
-    def store(n):
-        bands = pl.ds(2 * n, 2)
-        return pltpu.make_async_copy(xout.at[:, bands], out.at[:, bands], st_s.at[n])
 
     def gram_fields(q):
         await_bytes(xp.at[pl.ds(PART * q, PART)], xp_r.at[q])
-        x = [192 * h + 12 * b + PART * q + i for i in range(PART)]
+        x = [192 * h + ROWS * q + PART * b + i for i in range(PART)]
         gram(xp, q, [vxy[pl.ds(i, 1), :] for i in x])
 
     gram_fields(0)
     gram_fields(1)
     gram_fields(2)
+    each(0, 2, finish)
     gram_fields(3)
 
     gb[...] = gt[...].astype(BF)
@@ -446,7 +442,7 @@
     each(1, 16, lambda k: sb_send(band_peer(k)))
     local(gb.at[at(b, 16, 16), :], sb.at[b], sb_r.at[0])
     await_bytes(p2.at[pl.ds(0, 180)], xp_s.at[0])
-    each(0, 2, finish)
+    finish(2)
     await_bytes(sb, sb_r.at[0])
     total = sb[0].astype(F32)
     for k in range(1, 16):
@@ -460,7 +456,7 @@
 
     each(1, 8, lambda k: sa_send(ga_peer(k)))
     local(st.at[at(g, 32, 8), :], sa.at[g], sa_r.at[0])
-    each(2, 4, finish)
+    finish(3)
     await_bytes(w1.at[:, pl.ds(0, 7)], zo_s.at[0])
     await_bytes(sb.at[pl.ds(0, 15)], sb_s.at[0])
     await_bytes(sa, sa_r.at[0])
@@ -484,12 +480,6 @@
     sub[1] = ((ri[0:8] - rr[8:16]) * inverse_cells)[:, 0:16]
 
     await_bytes(sa.at[pl.ds(0, 7)], sa_s.at[0])
-    each(0, 4, lambda n: store(n).wait())
-
-
-def finished(rows, sums, out, sub):
-    out[...] = rows[...]
-    sub[...] = sums[...]
 
 
 def shards(table, waves, ionic_field, point_charge, charge_place, charge_slab):
@@ -500,12 +490,12 @@
     out, sub = pl.pallas_call(
         kernel,
         out_shape=(
-            jax.ShapeDtypeStruct((2, 8, 36, 16, 128), BF),
-            jax.ShapeDtypeStruct((2, 8, 16), F32),
+            vmem((2, 8, 36, 16, 128), BF),
+            vmem((2, 8, 16), F32),
         ),
         in_specs=[hbm] + [pl.BlockSpec(memory_space=pltpu.VMEM)] * 4 + [hbm],
         out_specs=(
-            hbm,
+            pl.BlockSpec(memory_space=pltpu.VMEM),
             pl.BlockSpec(memory_space=pltpu.VMEM),
         ),
         scratch_shapes=[
@@ -513,7 +503,6 @@
             vmem((2, 8, 4, ROWS, N), BF),
             vmem((2, N, N), F32),
             vmem((2, 8, 4, ROWS, N), BF),
-            vmem((2, 8, 36, 16, 128), BF),
             vmem((192, 192), BF),
             vmem((192, 192), BF),
             vmem((2 * N, 2 * N), BF),
@@ -560,7 +549,6 @@
             dma((1,)), dma((1,)),
             dma((1,)), dma((1,)),
             dma((5,)),
-            dma((4,)),
         ],
         compiler_params=pltpu.CompilerParams(
             collective_id=0, has_side_effects=True, vmem_limit_bytes=56 * 1024 * 1024
@@ -569,18 +557,6 @@
         tiled, point_charge.reshape(1, 256), charge_place, charge_slab.reshape(1, 256),
         ionic_field, table,
     )
-    halves = pl.BlockSpec((2, 4, 36, 16, 128), lambda i: (0, i, 0, 0, 0))
-    every = pl.BlockSpec((2, 8, 16), lambda i: (0, 0, 0))
-    out, sub = pl.pallas_call(
-        finished,
-        out_shape=(
-            jax.ShapeDtypeStruct((2, 8, 36, 16, 128), BF),
-            jax.ShapeDtypeStruct((2, 8, 16), F32),
-        ),
-        grid=(2,),
-        in_specs=[halves, every],
-        out_specs=(halves, every),
-    )(out, sub)
     out = out.reshape(2, 8, 144, 4, 128).transpose(0, 1, 3, 2, 4)
     return out.reshape(2, 8, 4, ROWS * N), sub
 

time: 88.3 us -> 87.2 us (0.988)
  Pallas kernels: 87.5 us -> 84.4 us
  local copies, waits for them, and re-layouts: 0 us -> 2.01 us
    pallas_call x2 -> x1, Pallas kernels: 87.5 us -> 84.4 us  [shards(): pl.pallas_call(kernel, out_shape=(vmem((2, 8, 36, 16, 128), BF), vmem((2,...]
    unnamed x0 -> x2, local copies, waits for them, and re-layouts: none -> 2.01 us
where the time goes in v4:
time: 87.2 us; the launch traced here: 87.1 us
  Pallas kernels  84.4 us (97%)
  local copies, waits for them, and re-layouts  2.01 us (2%)
    pallas_call x1, Pallas kernels, shards(): pl.pallas_call(kernel, out_shape=(vmem((2, 8, 36, 16, 128), BF), vmem((2,...  84.4 us
    unnamed x2, local copies, waits for them, and re-layouts  2.01 us

profile of v4, /device:TPU:1, one launch (start us, length us, event | category | flops | bytes accessed | tf_op | source)
XLA Modules:
  0.0 87.1 jit_solution(818616595626874237)
XLA Ops:
  0.6 84.4 %shard_map.77 = (bf16[2,8,36,16,128]{4,3,2,1,0:T(8,128)(2,1)S(1)}, f32[2,8,16]{2,1,0:T(8,128)S(1)}) custom-call(bf16[2,8,36,16,128]{4,3,2,1,0:T(8,128)(2,1)} %bitcast.13, f32[1,256]{1,0:T(1,128)} %bitcast.14, f32[3,256]{1,0:T(4,128)} %place.1, s32[1,256]{1,0:T(1,128)} %bitcast.15, f32[48,1536]{1,0:T(8,128)} %ionic.1, f32[2,384,384]{2,1,0:T(8,128)} %constant.2.clone.tab_in), custom_call_target="tpu_custom_call" | custom-call | tf_op jit(solution)/shard_map/pallas_call | solution.py:490
  85.0 1.4 %copy.12 = bf16[2,8,4,18432]{3,2,1,0:T(4,128)(2,1)} copy(bf16[2,8,4,18432]{3,2,1,0:T(4,128)(2,1)S(1)} %bitcast.12) | data formatting | bytes 4718592
  86.5 0.6 copy.13

commit v5 on v4

--- a/solution.py
+++ b/solution.py
@@ -71,7 +71,7 @@
 def kernel(
     waves, charge, place, slab_in, ionic, tab_in, out, sub,
     xin, w1, tab, rows_in, spread, gather, m1, m2, perm, kin, zb, w2, xw, phi, wide, ph, p2, xp, ab, fs, ts, bs,
-    chs, ch, ios, iop, pot, rsb, own, pf, vyx, vxy, gt, gb, sa, st, sb,
+    chs, ch, ios, iop, pot, pt, rsb, own, pf, vyx, vxy, gt, gb, sa, st, sb,
     zi_s, zi_r, zo_s, zo_r, ch_s, ch_r, io_s, io_r, rs_s, rs_r, ag_s, ag_r,
     sp_s, sp_r, sf_s, sf_r, xw_s, xw_r, xp_s, xp_r, sa_s, sa_r, sb_s, sb_r, loc,
 ):
@@ -217,7 +217,7 @@
             return src.at[pl.ds(ROWS * q + PART * target, PART)], dst.at[pl.ds(PART * q, PART), at(b, 16, 16), :]
 
         for dy, dx in SHIFTS:
-            target = shifted(dy, dx)
+            target = shifted(dy + h * (dx - dy), dx + h * (dy - dx))
             one, other = to(target)
             remote(one, other, send.at[0], recv.at[q], target, g).start()
         one, other = to(b)
@@ -226,9 +226,9 @@
     def sp_copy(half):
         return remote(pf.at[half], pf.at[half], sp_s.at[0], sp_r.at[0], b, sibling)
 
-    def sf_copy(n, core):
+    def sf_copy(n, part, core):
         return remote(
-            phi.at[n, :, at(1 - core, 192, 16), :], ph.at[:, 2 * n + core],
+            phi.at[n, part, at(1 - core, 192, 16), :], ph.at[part, 2 * n + core],
             sf_s.at[0], sf_r.at[n], b, sibling,
         )
 
@@ -303,13 +303,16 @@
 
     each(0, 4, add_two)
 
+    for j in range(16):
+        pt[j] = pot[16 * j : 16 * j + 12, :]
+
     def rs_send(target):
         remote(
-            pot.at[at(target, 16, 8), :], rsb.at[b], rs_s.at[0], rs_r.at[0], target, g
+            pt.at[target], rsb.at[b], rs_s.at[0], rs_r.at[0], target, g
         ).start()
 
     each(1, 16, lambda k: rs_send(band_peer(k)))
-    local(pot.at[at(b, 16, 8), :], rsb.at[b], rs_r.at[0])
+    local(pt.at[b], rsb.at[b], rs_r.at[0])
     send_waves(2)
 
     def forward(n):
@@ -321,7 +324,7 @@
             space = dot(m2[part * N : (part + 1) * N], fs[...])
             wide[n, part] = space
             phi[n, part] = space.astype(BF)
-        sf_copy(n, h).start()
+            sf_copy(n, part, h).start()
         for part in range(2):
             ph[part, 2 * n + h] = phi[n, part, at(h, 192, 16), :]
 
@@ -337,10 +340,10 @@
     def _():
         io_copy(z).wait_recv()
 
-    piece = iop[...]
+    piece = iop[0:12]
     for k in range(16):
         piece = piece + rsb[k]
-    own[...] = piece.astype(BF)
+    own[...] = jnp.concatenate([piece, jnp.zeros((4, N), F32)], axis=0).astype(BF)
 
     def ag_send(target):
         remote(own, pf.at[h, at(b, 16, 16), :], ag_s.at[0], ag_r.at[0], target, g).start()
@@ -349,10 +352,8 @@
     local(own, pf.at[h, at(b, 16, 16), :], ag_r.at[0])
     send_waves(3)
     each(2, 4, forward)
-    await_bytes(pf.at[h], ag_r.at[0])
-    sp_copy(h).start()
-
-    each(0, 4, lambda n: sf_copy(n, 1 - h).wait_recv())
+
+    each(0, 4, lambda n: await_bytes(ph.at[:, n], sf_r.at[n]))
 
     def turn_field(p):
         for x in range(3):
@@ -362,6 +363,9 @@
     for q in range(PARTS):
         turn_field(q)
         row_sends(q, p2, xp, xp_s, xp_r)
+        if q == 1:
+            await_bytes(pf.at[h], ag_r.at[0])
+            sp_copy(h).start()
 
     sp_copy(1 - h).wait_recv()
     for half in range(2):
@@ -526,7 +530,8 @@
             vmem((4, 16, N), F32),
             vmem((16, N), F32),
             vmem((256, N), F32),
-            vmem((16, 16, N), F32),
+            vmem((16, 12, N), F32),
+            vmem((16, 12, N), F32),
             vmem((16, N), BF),
             vmem((2, 256, N), BF),
             vmem((N, N), F32),

time: 87.2 us -> 87 us (level)
  no operation moved by 1% of the time
where the time goes in v5:
time: 87 us; the launch traced here: 86.8 us
  Pallas kernels  84.2 us (97%)
  local copies, waits for them, and re-layouts  2.01 us (2%)
    pallas_call x1, Pallas kernels, shards(): pl.pallas_call(kernel, out_shape=(vmem((2, 8, 36, 16, 128), BF), vmem((2,...  84.2 us
    unnamed x2, local copies, waits for them, and re-layouts  2.01 us

profile of v5, /device:TPU:1, one launch (start us, length us, event | category | flops | bytes accessed | tf_op | source)
XLA Modules:
  0.0 86.8 jit_solution(1190426312722447840)
XLA Ops:
  0.6 84.2 %shard_map.77 = (bf16[2,8,36,16,128]{4,3,2,1,0:T(8,128)(2,1)S(1)}, f32[2,8,16]{2,1,0:T(8,128)S(1)}) custom-call(bf16[2,8,36,16,128]{4,3,2,1,0:T(8,128)(2,1)} %bitcast.13, f32[1,256]{1,0:T(1,128)} %bitcast.14, f32[3,256]{1,0:T(4,128)} %place.1, s32[1,256]{1,0:T(1,128)} %bitcast.15, f32[48,1536]{1,0:T(8,128)} %ionic.1, f32[2,384,384]{2,1,0:T(8,128)} %constant.2.clone.tab_in), custom_call_target="tpu_custom_call" | custom-call | tf_op jit(solution)/shard_map/pallas_call | solution.py:494
  84.8 1.4 %copy.12 = bf16[2,8,4,18432]{3,2,1,0:T(4,128)(2,1)} copy(bf16[2,8,4,18432]{3,2,1,0:T(4,128)(2,1)S(1)} %bitcast.12) | data formatting | bytes 4718592
  86.2 0.6 copy.13

commit v6 on v5

--- a/solution.py
+++ b/solution.py
@@ -179,7 +179,6 @@
             turned = dot(perm[...], block).astype(BF).reshape(16, 16, N)
             w2[pl.ds(ROWS * p + 16 * x, 16)] = turned
 
-    each(0, 4, turn)
     pl.semaphore_wait(barrier, 22)
 
     def local(src, dst, sem):
@@ -243,9 +242,12 @@
     def send_waves(q):
         row_sends(q, w2, xw, xw_s, xw_r)
 
+    turn(0)
     send_waves(0)
+    each(1, 4, zi_all)
+    turn(1)
     send_waves(1)
-    each(1, 4, zi_all)
+    each(2, 4, turn)
 
     @pl.when(io_sends)
     def _():
@@ -451,22 +453,22 @@
     total = sb[0].astype(F32)
     for k in range(1, 16):
         total = total + sb[k].astype(F32)
-    st[...] = jnp.concatenate([total, jnp.zeros((112, 256), F32)], axis=0).T
+    st[...] = jnp.concatenate([total, jnp.zeros((112, 256), F32)], axis=0).T.astype(BF)
 
     def sa_send(target):
         remote(
-            st.at[at(target, 32, 8), :], sa.at[g], sa_s.at[0], sa_r.at[0], b, target
+            st.at[at(target, 32, 16), :], sa.at[g], sa_s.at[0], sa_r.at[0], b, target
         ).start()
 
     each(1, 8, lambda k: sa_send(ga_peer(k)))
-    local(st.at[at(g, 32, 8), :], sa.at[g], sa_r.at[0])
+    local(st.at[at(g, 32, 16), :], sa.at[g], sa_r.at[0])
     finish(3)
     await_bytes(w1.at[:, pl.ds(0, 7)], zo_s.at[0])
     await_bytes(sb.at[pl.ds(0, 15)], sb_s.at[0])
     await_bytes(sa, sa_r.at[0])
-    block = sa[0]
+    block = sa[0].astype(F32)
     for k in range(1, 8):
-        block = block + sa[k]
+        block = block + sa[k].astype(F32)
     block = jnp.concatenate([block, jnp.zeros((96, 128), F32)], axis=0).T[0:16]
     row = lax.broadcasted_iota(jnp.int32, (128, 128), 0)
     col = lax.broadcasted_iota(jnp.int32, (128, 128), 1)
@@ -538,8 +540,8 @@
             vmem((N, N), F32),
             vmem((256, 256), F32),
             vmem((256, 256), BF),
-            vmem((8, 32, 128), F32),
-            vmem((256, 128), F32),
+            vmem((8, 32, 128), BF),
+            vmem((256, 128), BF),
             vmem((16, 16, 256), BF),
             dma((1,)), dma((4,)),
             dma((1,)), dma((4,)),

time: 87 us -> 86.5 us (level)
  no operation moved by 1% of the time
where the time goes in v6:
time: 86.5 us; the launch traced here: 86.4 us
  Pallas kernels  83.7 us (97%)
  local copies, waits for them, and re-layouts  2.01 us (2%)
    pallas_call x1, Pallas kernels, shards(): pl.pallas_call(kernel, out_shape=(vmem((2, 8, 36, 16, 128), BF), vmem((2,...  83.7 us
    unnamed x2, local copies, waits for them, and re-layouts  2.01 us

profile of v6, /device:TPU:1, one launch (start us, length us, event | category | flops | bytes accessed | tf_op | source)
XLA Modules:
  0.0 86.4 jit_solution(11803760469397129596)
XLA Ops:
  0.6 83.7 %shard_map.77 = (bf16[2,8,36,16,128]{4,3,2,1,0:T(8,128)(2,1)S(1)}, f32[2,8,16]{2,1,0:T(8,128)S(1)}) custom-call(bf16[2,8,36,16,128]{4,3,2,1,0:T(8,128)(2,1)} %bitcast.13, f32[1,256]{1,0:T(1,128)} %bitcast.14, f32[3,256]{1,0:T(4,128)} %place.1, s32[1,256]{1,0:T(1,128)} %bitcast.15, f32[48,1536]{1,0:T(8,128)} %ionic.1, f32[2,384,384]{2,1,0:T(8,128)} %constant.2.clone.tab_in), custom_call_target="tpu_custom_call" | custom-call | tf_op jit(solution)/shard_map/pallas_call | solution.py:496
  84.4 1.4 %copy.12 = bf16[2,8,4,18432]{3,2,1,0:T(4,128)(2,1)} copy(bf16[2,8,4,18432]{3,2,1,0:T(4,128)(2,1)S(1)} %bitcast.12) | data formatting | bytes 4718592
  85.8 0.6 copy.13
